TPU v7x, 128 devices: a whole 4x4x4 slice. The times are simulated.
128 devices in a mesh: ha: 4 (over y_hi, core), wa: 32 (over y_lo, x, z).
Axes of the slice: x: 4, y: 4 (y_hi: 2, y_lo: 2; y = y_hi * 2 + y_lo), z: 4, core: 2. Of those that a mesh axis runs over, the one named last changes fastest.
Arguments:
- queries: bfloat16 [8, 32, 384, 1536], P('ha', 'wa'), may hold values from -8 to 8
- keys: bfloat16 [8, 32, 384, 1536], P('ha', 'wa'), may hold values from -8 to 8
- values: bfloat16 [8, 32, 384, 1536], P('ha', 'wa'), may hold values from -6 to 6
- selected: int32 [8, 32, 32], P('ha', 'wa'), may hold values from 0 to 767, as said below
- counts: int32 [8, 32], P('ha', 'wa'), may hold values from 16 to 32, as said below
Outputs:
- mixed: bfloat16 [8, 32, 384, 1536], P('ha', 'wa')
Inputs may be any that keep to these rules, and one draw needn't show every extreme that they name: `selected`: Of the 64 entries of one device's tiles, live or not, at most 2 name cubes of any one column, and in every band one column is named by exactly 2 entries of every device of the band. Only the first counts entries of a tile's list are live; some tile has all 32 live.
All inputs are finite; a program needn't handle non-finite values.
Results may differ from a plain program's by a relative error of at most 0.0035.
Values may be sent and summed in bfloat16 or wider, within the bound.
No kernel may reach another device: no remote copies, remote signals or barrier semaphores. Data moves between devices by JAX's collectives and lax.ppermute only.
A program may use at most 256 MiB of HBM per device.

v0:
```python
import math

import jax
import jax.numpy as jnp
from jax import lax
from jax.sharding import PartitionSpec as P

HEAD = 128
CUBE = 32


def with_halo(value, sides, width):
    for axis, dim in sides:
        size, length = (lax.axis_size(axis), value.shape[dim])
        up = [(i, (i + 1) % size) for i in range(size - 1)]
        down = [(j, i) for i, j in up]
        last = lax.slice_in_dim(value, length - width, length, axis=dim)
        first = lax.slice_in_dim(value, 0, width, axis=dim)
        before = lax.ppermute(last, axis, up)
        after = lax.ppermute(first, axis, down)
        value = jnp.concatenate([before, value, after], axis=dim)
    return value


def attend(query_tile, all_keys, all_vals, usable, head_size):
    tile_len = query_tile.shape[0]
    features = query_tile.shape[1]
    key_len = all_keys.shape[0]
    heads = features // head_size
    group_size = math.gcd(heads, 4)
    span = group_size * head_size
    score_scale = float(head_size) ** (-0.5)

    def one_group(group_idx):
        begin = group_idx * span
        query_part = lax.dynamic_slice_in_dim(query_tile, begin, span, 1).reshape(
            tile_len, group_size, head_size
        )
        key_part = lax.dynamic_slice_in_dim(all_keys, begin, span, 1).reshape(
            key_len, group_size, head_size
        )
        val_part = lax.dynamic_slice_in_dim(all_vals, begin, span, 1).reshape(
            key_len, group_size, head_size
        )
        scores = (
            jnp.einsum("qgd,kgd->gqk", query_part, key_part, preferred_element_type=jnp.float32)
            * score_scale
        )
        scores = jnp.where(usable[None, None, :], scores, -jnp.inf)
        row_max = jnp.max(scores, axis=-1, keepdims=True)
        weights = jnp.exp(scores - row_max)
        totals = jnp.sum(weights, axis=-1)
        rounded = weights.astype(jnp.bfloat16)
        mixed = jnp.einsum("gqk,kgd->qgd", rounded, val_part, preferred_element_type=jnp.float32)
        mixed = mixed / jnp.transpose(totals)[:, :, None]
        return mixed.astype(jnp.bfloat16).reshape(tile_len, span)

    groups = lax.map(one_group, jnp.arange(heads // group_size, dtype=jnp.int32))
    return jnp.transpose(groups, (1, 0, 2)).reshape(tile_len, features)


def body(queries, keys, values, selected, counts):
    tile_rows = queries.shape[0]
    tile_len = queries.shape[2]
    features = queries.shape[3]
    slots_tile = selected.shape[2]
    cube_len = CUBE
    head_size = HEAD
    cubes_dev = tile_rows * (tile_len // cube_len)
    columns = lax.axis_size("wa")
    rows_total = lax.axis_size("ha") * tile_rows
    capacity = max(2, -(-(tile_rows * slots_tile) // columns))
    paired = jnp.stack([keys, values])
    extended = with_halo(paired, (("ha", 1), ("wa", 2)), 1)
    flat_ids = selected.reshape(tile_rows * slots_tile)
    owners = flat_ids // cubes_dev
    local_ids = flat_ids % cubes_dev
    onehot = (owners[:, None] == jnp.arange(columns, dtype=jnp.int32)[None, :]).astype(jnp.int32)
    slot_rank = jnp.sum(jnp.cumsum(onehot, axis=0) * onehot, axis=1) - 1
    requests = jnp.zeros((columns, capacity), jnp.int32).at[owners, slot_rank].set(local_ids)
    key_table = keys.reshape(cubes_dev, cube_len, features)
    val_table = values.reshape(cubes_dev, cube_len, features)
    asked_ids = lax.all_to_all(requests, "wa", split_axis=0, concat_axis=0, tiled=True)
    found_keys = key_table[asked_ids]
    found_vals = val_table[asked_ids]
    fetched_keys, fetched_vals = (
        lax.all_to_all(found_keys, "wa", split_axis=0, concat_axis=0, tiled=True),
        lax.all_to_all(found_vals, "wa", split_axis=0, concat_axis=0, tiled=True),
    )
    slot_keys = fetched_keys[owners, slot_rank].reshape(tile_rows, slots_tile * cube_len, features)
    slot_vals = fetched_vals[owners, slot_rank].reshape(tile_rows, slots_tile * cube_len, features)
    live_slots = jnp.arange(slots_tile, dtype=jnp.int32)[None, :] < counts[:, 0][:, None]
    live_slots = jnp.repeat(live_slots, cube_len, axis=1)
    base_row = lax.axis_index("ha") * tile_rows
    base_col = lax.axis_index("wa")
    row_pos = base_row + jnp.arange(tile_rows + 2, dtype=jnp.int32) - 1
    col_pos = base_col + jnp.arange(3, dtype=jnp.int32) - 1
    row_ok = (row_pos >= 0) & (row_pos < rows_total)
    col_ok = (col_pos >= 0) & (col_pos < columns)
    outputs = []
    for row_idx in range(tile_rows):
        win_keys = extended[0, row_idx : row_idx + 3].reshape(9 * tile_len, features)
        win_vals = extended[1, row_idx : row_idx + 3].reshape(9 * tile_len, features)
        window_ok = jnp.repeat(
            (row_ok[row_idx : row_idx + 3, None] & col_ok[None, :]).reshape(9), tile_len
        )
        all_keys = jnp.concatenate([win_keys, slot_keys[row_idx]], axis=0)
        all_vals = jnp.concatenate([win_vals, slot_vals[row_idx]], axis=0)
        usable = jnp.concatenate([window_ok, live_slots[row_idx]], axis=0)
        outputs.append(attend(queries[row_idx, 0], all_keys, all_vals, usable, head_size))
    return jnp.stack(outputs)[:, None]


def solution(mesh):
    return jax.shard_map(
        body,
        mesh=mesh,
        in_specs=(
            P("ha", "wa", None, None),
            P("ha", "wa", None, None),
            P("ha", "wa", None, None),
            P("ha", "wa", None),
            P("ha", "wa"),
        ),
        out_specs=P("ha", "wa", None, None),
        check_vma=False,
    )
```

profile of v0, /device:TPU:7, one launch (start us, length us, event | category | flops | bytes accessed | tf_op | source)
XLA Modules:
  0.0 1037.6 jit_solution(10790169602365296838)
XLA Ops:
  7.0 14.2 %all_to_all.22 = s32[32,1,2]{2,1,0:T(1,128)S(1)} all-to-all(s32[32,1,2]{2,1,0:T(1,128)S(1)} %copy.43), channel_id=1, replica_groups=mesh['ha'=4,'wa'=32] {'wa'}, dimensions={0} | all-to-all | bytes 512 | tf_op jit(solution)/shard_map/all_to_all | solution.py:83
  44.0 87.5 %collective-permute-done = bf16[2,1,1,384,1536]{4,3,2,1,0:T(8,128)(2,1)S(1)} collective-permute-done((bf16[2,1,1,384,1536]{4,3,2,1,0:T(8,128)(2,1)S(1)}, bf16[2,1,1,384,1536]{4,3,2,1,0:T(8,128)(2,1)S(1)}, u32[]{:S(2)}, u32[]{:S(2)}) %collective-permute-start) | collective-permute-done | bytes 2359328 | tf_op jit(solution)/shard_map/ppermute | solution.py:19
  156.7 155.2 %all-to-all-done.2 = bf16[32,2,32,1536]{3,2,1,0:T(8,128)(2,1)} async-done(((bf16[32,2,32,1536]{3,2,1,0:T(8,128)(2,1)}), bf16[32,2,32,1536]{3,2,1,0:T(8,128)(2,1)}, u32[]{:S(2)}, u32[]{:S(2)}) %all-to-all-start.2) | async-done | bytes 6291488 | tf_op jit(solution)/shard_map/all_to_all | solution.py:87
  312.0 89.1 %all-to-all-start.1 = ((bf16[32,2,32,1536]{3,2,1,0:T(8,128)(2,1)}), bf16[32,2,32,1536]{3,2,1,0:T(8,128)(2,1)}, u32[]{:S(2)}, u32[]{:S(2)}) async-start(bf16[32,2,32,1536]{3,2,1,0:T(8,128)(2,1)} %bitcast.148), calls=%async_computation.1 | async-start | bytes 12582912 | tf_op jit(solution)/shard_map/all_to_all | solution.py:88
  436.1 124.9 %all-to-all-done.1 = bf16[32,2,32,1536]{3,2,1,0:T(8,128)(2,1)} async-done(((bf16[32,2,32,1536]{3,2,1,0:T(8,128)(2,1)}), bf16[32,2,32,1536]{3,2,1,0:T(8,128)(2,1)}, u32[]{:S(2)}, u32[]{:S(2)}) %all-to-all-start.1) | async-done | bytes 6291488 | tf_op jit(solution)/shard_map/all_to_all | solution.py:88
  573.5 19.5 %pad_maximum_fusion = bf16[2,4,3,384,1536]{4,3,2,1,0:T(8,128)(2,1)} fusion(bf16[2,4,1,384,1536]{4,3,2,1,0:T(8,128)(2,1)} %collective-permute-done.3, bf16[2,1,1,384,1536]{4,3,2,1,0:T(8,128)(2,1)} %copy-done.9, bf16[1,2,1,384,1536]{4,3,2,1,0:T(8,128)(2,1)S(1)} %bitcast.137, bf16[1,2,1,384,1536]{4,3,2,1,0:T(8,128)(2,1)} %bitcast.140, ...), kind=kLoop, calls=%fused_computation.37 | loop fusion | flops 70778880 | bytes 56623104 | tf_op jit(solution)/shard_map/concatenate | solution.py:21
  593.0 27.4 %fusion.40 = (bf16[1,3,3,384,1536]{4,3,2,1,0:T(8,128)(2,1)}, bf16[1,3,3,384,1536]{4,3,2,1,0:T(8,128)(2,1)}, bf16[1,3,3,384,1536]{4,3,2,1,0:T(8,128)(2,1)}, bf16[1,3,3,384,1536]{4,3,2,1,0:T(8,128)(2,1)}) fusion(bf16[2,4,3,384,1536]{4,3,2,1,0:T(8,128)(2,1)} %pad_maximum_fusion), kind=kLoop, calls=%fused_computation.78 | loop fusion | bytes 84934656 | tf_op jit(solution)/shard_map/slice | solution.py:102
  620.4 13.9 %copy.47 = bf16[3456,1536]{0,1:T(8,128)(2,1)} copy(bf16[3456,1536]{1,0:T(8,128)(2,1)} %bitcast.145) | data formatting | bytes 21233664 | tf_op jit(solution)/shard_map/reshape;squeeze | solution.py:102
  634.4 14.3 %pad_maximum_fusion.2 = bf16[4480,1536]{0,1:T(8,128)(2,1)} fusion(bf16[1024,1536]{0,1:T(8,128)(2,1)S(1)} %copy-done.5, bf16[3456,1536]{0,1:T(8,128)(2,1)} %copy.47), kind=kLoop, calls=%fused_computation.39 | loop fusion | flops 27525120 | bytes 27525120 | tf_op jit(solution)/shard_map/concatenate | solution.py:107
  648.7 17.0 %pad_maximum_fusion.1 = bf16[4480,1536]{1,0:T(8,128)(2,1)} fusion(bf16[1024,1536]{1,0:T(8,128)(2,1)S(1)} %bitcast.153, bf16[3456,1536]{1,0:T(8,128)(2,1)S(1)} %bitcast.144), kind=kLoop, calls=%fused_computation.38 | loop fusion | flops 27525120 | bytes 27525120 | tf_op jit(solution)/shard_map/concatenate | solution.py:108
  665.8 160.7 %while.20 = (s32[]{:T(128)}, bf16[3,384,512]{1,2,0:T(8,128)(2,1)S(1)}, s32[3]{0:T(128)S(1)}, bf16[4480,1536]{1,0:T(8,128)(2,1)}, pred[4480]{0:T(1024)(128)(4,1)S...) while((s32[]{:T(128)}, ...), condition=%wide.region_6.7_spmd, body=%wide.region_3.6_spmd.sunk | while | flops 3599299584 | bytes 121679152 | solution.py:58
  706.0 13.4 %fusion.71 = bf16[384,4,128]{0,2,1:T(8,128)(2,1)S(1)} fusion(bf16[4480,4,128]{0,2,1:T(8,128)(2,1)} %bitcast.132, f32[4,384,4480]{2,1,0:T(8,128)} %get-tuple-element.266, f32[4,384]{1,0:T(4,128)S(1)} %get-tuple-element.267, pred[4480]{0:T(1024)(128)(4,1)S(1)} %get-tuple-element.336, f32[384,4]{0,1:T(4,128)S(1)} %bitcast.160), kind=kOutput, calls=%fused_computation.14.clone.1 | convolution fusion | flops 1789526016 | bytes 32522624 | tf_op jit(solution)/shard_map/while/body/eval_jaxpr/gqk,kgd->qgd/dot_general | solution.py:54
  759.5 13.4 %fusion.71 = bf16[384,4,128]{0,2,1:T(8,128)(2,1)S(1)} fusion(bf16[4480,4,128]{0,2,1:T(8,128)(2,1)} %bitcast.132, f32[4,384,4480]{2,1,0:T(8,128)} %get-tuple-element.266, f32[4,384]{1,0:T(4,128)S(1)} %get-tuple-element.267, pred[4480]{0:T(1024)(128)(4,1)S(1)} %get-tuple-element.336, f32[384,4]{0,1:T(4,128)S(1)} %bitcast.160), kind=kOutput, calls=%fused_computation.14.clone.1 | convolution fusion | flops 1789526016 | bytes 32522624 | tf_op jit(solution)/shard_map/while/body/eval_jaxpr/gqk,kgd->qgd/dot_general | solution.py:54
  813.0 13.4 %fusion.71 = bf16[384,4,128]{0,2,1:T(8,128)(2,1)S(1)} fusion(bf16[4480,4,128]{0,2,1:T(8,128)(2,1)} %bitcast.132, f32[4,384,4480]{2,1,0:T(8,128)} %get-tuple-element.266, f32[4,384]{1,0:T(4,128)S(1)} %get-tuple-element.267, pred[4480]{0:T(1024)(128)(4,1)S(1)} %get-tuple-element.336, f32[384,4]{0,1:T(4,128)S(1)} %bitcast.160), kind=kOutput, calls=%fused_computation.14.clone.1 | convolution fusion | flops 1789526016 | bytes 32522624 | tf_op jit(solution)/shard_map/while/body/eval_jaxpr/gqk,kgd->qgd/dot_general | solution.py:54
  827.5 14.1 %copy.51 = bf16[3456,1536]{0,1:T(8,128)(2,1)} copy(bf16[3456,1536]{1,0:T(8,128)(2,1)} %bitcast.143) | data formatting | bytes 21233664 | tf_op jit(solution)/shard_map/reshape;squeeze | solution.py:102
  841.6 14.3 %pad_maximum_fusion.4 = bf16[4480,1536]{0,1:T(8,128)(2,1)} fusion(bf16[1024,1536]{0,1:T(8,128)(2,1)S(1)} %copy-done.4, bf16[3456,1536]{0,1:T(8,128)(2,1)} %copy.51), kind=kLoop, calls=%fused_computation.41 | loop fusion | flops 27525120 | bytes 27525120 | tf_op jit(solution)/shard_map/concatenate | solution.py:107
  855.9 17.0 %pad_maximum_fusion.3 = bf16[4480,1536]{1,0:T(8,128)(2,1)} fusion(bf16[1024,1536]{1,0:T(8,128)(2,1)S(1)} %bitcast.152, bf16[3456,1536]{1,0:T(8,128)(2,1)S(1)} %bitcast.142), kind=kLoop, calls=%fused_computation.40 | loop fusion | flops 27525120 | bytes 27525120 | tf_op jit(solution)/shard_map/concatenate | solution.py:108
  873.0 160.5 %while.21 = (s32[]{:T(128)}, bf16[3,384,512]{1,2,0:T(8,128)(2,1)S(1)}, s32[3]{0:T(128)S(1)}, bf16[4480,1536]{1,0:T(8,128)(2,1)}, pred[4480]{0:T(1024)(128)(4,1)S...) while((s32[]{:T(128)}, ...), condition=%wide.region_10.11_spmd, body=%wide.region_7.10_spmd.sunk | while | flops 3599299584 | bytes 121679152 | solution.py:58
  889.5 12.5 %fusion.77 = f32[4,384]{1,0:T(4,128)S(1)} fusion(f32[4,384,4480]{2,1,0:T(8,128)} %get-tuple-element.275, f32[4,384]{1,0:T(4,128)S(1)} %get-tuple-element.276, pred[4480]{0:T(1024)(128)(4,1)S(1)} %get-tuple-element.303), kind=kLoop, calls=%fused_computation.24.clone.1 | loop fusion | flops 27523584 | bytes 27541888 | tf_op jit(solution)/shard_map/while/body/eval_jaxpr/reduce_sum | solution.py:52
  913.4 13.2 %fusion.78 = bf16[384,4,128]{0,2,1:T(8,128)(2,1)S(1)} fusion(bf16[4480,4,128]{0,2,1:T(8,128)(2,1)} %bitcast.133, f32[4,384,4480]{2,1,0:T(8,128)} %get-tuple-element.275, f32[4,384]{1,0:T(4,128)S(1)} %get-tuple-element.276, pred[4480]{0:T(1024)(128)(4,1)S(1)} %get-tuple-element.303, f32[384,4]{0,1:T(4,128)S(1)} %bitcast.161), kind=kOutput, calls=%fused_computation.30.clone.1 | convolution fusion | flops 1789526016 | bytes 32522624 | tf_op jit(solution)/shard_map/while/body/eval_jaxpr/gqk,kgd->qgd/dot_general | solution.py:54
  942.9 12.5 %fusion.77 = f32[4,384]{1,0:T(4,128)S(1)} fusion(f32[4,384,4480]{2,1,0:T(8,128)} %get-tuple-element.275, f32[4,384]{1,0:T(4,128)S(1)} %get-tuple-element.276, pred[4480]{0:T(1024)(128)(4,1)S(1)} %get-tuple-element.303), kind=kLoop, calls=%fused_computation.24.clone.1 | loop fusion | flops 27523584 | bytes 27541888 | tf_op jit(solution)/shard_map/while/body/eval_jaxpr/reduce_sum | solution.py:52
  966.8 13.2 %fusion.78 = bf16[384,4,128]{0,2,1:T(8,128)(2,1)S(1)} fusion(bf16[4480,4,128]{0,2,1:T(8,128)(2,1)} %bitcast.133, f32[4,384,4480]{2,1,0:T(8,128)} %get-tuple-element.275, f32[4,384]{1,0:T(4,128)S(1)} %get-tuple-element.276, pred[4480]{0:T(1024)(128)(4,1)S(1)} %get-tuple-element.303, f32[384,4]{0,1:T(4,128)S(1)} %bitcast.161), kind=kOutput, calls=%fused_computation.30.clone.1 | convolution fusion | flops 1789526016 | bytes 32522624 | tf_op jit(solution)/shard_map/while/body/eval_jaxpr/gqk,kgd->qgd/dot_general | solution.py:54
  996.3 12.5 %fusion.77 = f32[4,384]{1,0:T(4,128)S(1)} fusion(f32[4,384,4480]{2,1,0:T(8,128)} %get-tuple-element.275, f32[4,384]{1,0:T(4,128)S(1)} %get-tuple-element.276, pred[4480]{0:T(1024)(128)(4,1)S(1)} %get-tuple-element.303), kind=kLoop, calls=%fused_computation.24.clone.1 | loop fusion | flops 27523584 | bytes 27541888 | tf_op jit(solution)/shard_map/while/body/eval_jaxpr/reduce_sum | solution.py:52
  1020.2 13.2 %fusion.78 = bf16[384,4,128]{0,2,1:T(8,128)(2,1)S(1)} fusion(bf16[4480,4,128]{0,2,1:T(8,128)(2,1)} %bitcast.133, f32[4,384,4480]{2,1,0:T(8,128)} %get-tuple-element.275, f32[4,384]{1,0:T(4,128)S(1)} %get-tuple-element.276, pred[4480]{0:T(1024)(128)(4,1)S(1)} %get-tuple-element.303, f32[384,4]{0,1:T(4,128)S(1)} %bitcast.161), kind=kOutput, calls=%fused_computation.30.clone.1 | convolution fusion | flops 1789526016 | bytes 32522624 | tf_op jit(solution)/shard_map/while/body/eval_jaxpr/gqk,kgd->qgd/dot_general | solution.py:54
  (136 shorter events, 307.0 us)
Async XLA Ops:
  26.8 6.5 copy-start
  26.8 285.2 %all-to-all-start.2 = ((bf16[32,2,32,1536]{3,2,1,0:T(8,128)(2,1)}), bf16[32,2,32,1536]{3,2,1,0:T(8,128)(2,1)}, u32[]{:S(2)}, u32[]{:S(2)}) async-start(bf16[32,2,32,1536]{3,2,1,0:T(8,128)(2,1)} %bitcast.149), calls=%async_computation.2 | async-start | bytes 12582912 | tf_op jit(solution)/shard_map/all_to_all | solution.py:87
  33.3 101.7 %copy-start.1 = (bf16[2,1,384,1536]{3,2,1,0:T(8,128)(2,1)S(1)}, bf16[2,1,384,1536]{3,2,1,0:T(8,128)(2,1)}, u32[]{:S(2)}) copy-start(bf16[2,1,384,1536]{3,2,1,0:T(8,128)(2,1)} %param.10) | copy-start | bytes 7077892
  35.3 96.2 %collective-permute-start = (bf16[2,1,1,384,1536]{4,3,2,1,0:T(8,128)(2,1)S(1)}, bf16[2,1,1,384,1536]{4,3,2,1,0:T(8,128)(2,1)S(1)}, u32[]{:S(2)}, u32[]{:S(2)}) collective-permute-start(bf16[2,1,1,384,1536]{4,3,2,1,0:T(8,128)(2,1)S(1)} %get-tuple-element.167), channel_id=1, source_target_pairs={{0,32},{32,64},{64,96},{1,33},{33,65},{65,97},{2,34},{34,66},{66,9... | collective-permute-start | bytes 7077896 | tf_op jit(solution)/shard_map/ppermute | solution.py:19
  42.1 92.8 %collective-permute-start.1 = (bf16[2,1,1,384,1536]{4,3,2,1,0:T(8,128)(2,1)S(1)}, bf16[2,1,1,384,1536]{4,3,2,1,0:T(8,128)(2,1)S(1)}, u32[]{:S(2)}, u32[]{:S(2)}) collective-permute-start(bf16[2,1,1,384,1536]{4,3,2,1,0:T(8,128)(2,1)S(1)} %get-tuple-element.168), channel_id=1, source_target_pairs={{32,0},{64,32},{96,64},{33,1},{65,33},{97,65},{34,2},{66,34},{98,6... | collective-permute-start | bytes 7077896 | tf_op jit(solution)/shard_map/ppermute | solution.py:20
  131.5 8.3 copy-start.8
  134.9 4.8 copy-start.9
  139.8 433.7 %collective-permute-start.2 = (bf16[2,4,1,384,1536]{4,3,2,1,0:T(8,128)(2,1)}, bf16[2,4,1,384,1536]{4,3,2,1,0:T(8,128)(2,1)}, u32[]{:S(2)}, u32[]{:S(2)}) collective-permute-start(bf16[2,4,1,384,1536]{4,3,2,1,0:T(8,128)(2,1)} %pad_maximum_fusion.5), channel_id=1, source_target_pairs={{0,1},{1,2},{2,3},{3,4},{4,5},{5,6},{6,7},{7,8},{8,9},{9,10},{10,1... | collective-permute-start | bytes 28311560 | tf_op jit(solution)/shard_map/ppermute | solution.py:19
  143.5 430.0 %collective-permute-start.3 = (bf16[2,4,1,384,1536]{4,3,2,1,0:T(8,128)(2,1)}, bf16[2,4,1,384,1536]{4,3,2,1,0:T(8,128)(2,1)}, u32[]{:S(2)}, u32[]{:S(2)}) collective-permute-start(bf16[2,4,1,384,1536]{4,3,2,1,0:T(8,128)(2,1)} %pad_maximum_fusion.5), channel_id=1, source_target_pairs={{1,0},{2,1},{3,2},{4,3},{5,4},{6,5},{7,6},{8,7},{9,8},{10,9},{11,1... | collective-permute-start | bytes 28311560 | tf_op jit(solution)/shard_map/ppermute | solution.py:20
  156.7 244.8 %copy-start.12 = (s32[2,1]{0,1:T(1,128)S(1)}, s32[2,1]{0,1:T(1,128)}, u32[]{:S(2)}) copy-start(s32[2,1]{0,1:T(1,128)} %param.13) | copy-start | bytes 28
  312.0 249.0 %all-to-all-start.1 = ((bf16[32,2,32,1536]{3,2,1,0:T(8,128)(2,1)}), bf16[32,2,32,1536]{3,2,1,0:T(8,128)(2,1)}, u32[]{:S(2)}, u32[]{:S(2)}) async-start(bf16[32,2,32,1536]{3,2,1,0:T(8,128)(2,1)} %bitcast.148), calls=%async_computation.1 | async-start | bytes 12582912 | tf_op jit(solution)/shard_map/all_to_all | solution.py:88
  620.4 13.9 %copy-start.5 = (bf16[1024,1536]{0,1:T(8,128)(2,1)S(1)}, bf16[1024,1536]{0,1:T(8,128)(2,1)}, u32[]{:S(2)}) copy-start(bf16[1024,1536]{0,1:T(8,128)(2,1)} %copy.48) | copy-start | bytes 9437188
  634.3 14.3 %copy-start.3 = (bf16[1,3,3,384,1536]{4,3,2,1,0:T(8,128)(2,1)S(1)}, bf16[1,3,3,384,1536]{4,3,2,1,0:T(8,128)(2,1)}, u32[]{:S(2)}) copy-start(bf16[1,3,3,384,1536]{4,3,2,1,0:T(8,128)(2,1)} %get-tuple-element.162) | copy-start | bytes 31850500
  634.3 14.3 %copy-start.7 = (bf16[32,32,1536]{2,1,0:T(8,128)(2,1)S(1)}, bf16[32,32,1536]{2,1,0:T(8,128)(2,1)}, u32[]{:S(2)}) copy-start(bf16[32,32,1536]{2,1,0:T(8,128)(2,1)} %get-tuple-element.165) | copy-start | bytes 9437188
  826.5 1.0 copy-start.10
  827.5 14.1 %copy-start.4 = (bf16[1024,1536]{0,1:T(8,128)(2,1)S(1)}, bf16[1024,1536]{0,1:T(8,128)(2,1)}, u32[]{:S(2)}) copy-start(bf16[1024,1536]{0,1:T(8,128)(2,1)} %copy.52) | copy-start | bytes 9437188
  841.6 14.3 %copy-start.2 = (bf16[1,3,3,384,1536]{4,3,2,1,0:T(8,128)(2,1)S(1)}, bf16[1,3,3,384,1536]{4,3,2,1,0:T(8,128)(2,1)}, u32[]{:S(2)}) copy-start(bf16[1,3,3,384,1536]{4,3,2,1,0:T(8,128)(2,1)} %get-tuple-element.161) | copy-start | bytes 31850500
  841.6 14.3 %copy-start.6 = (bf16[32,32,1536]{2,1,0:T(8,128)(2,1)S(1)}, bf16[32,32,1536]{2,1,0:T(8,128)(2,1)}, u32[]{:S(2)}) copy-start(bf16[32,32,1536]{2,1,0:T(8,128)(2,1)} %get-tuple-element.166) | copy-start | bytes 9437188
  855.9 17.1 %copy-start.11 = (pred[4480]{0:T(1024)(128)(4,1)S(1)}, pred[4480]{0:T(1024)(128)(4,1)}, u32[]{:S(2)}) copy-start(pred[4480]{0:T(1024)(128)(4,1)} %pad_add_fusion.1) | copy-start | bytes 13444
where the time goes:
time: 1040 us
  waiting for transfers between devices  371 us (36%)
  local copies, waits for them, and re-layouts  212 us (20%)
  other arithmetic  170 us (16%)
  matrix products  148 us (14%)
  starting transfers between devices  118 us (11%)
  blocking collectives  14.2 us (1%)
    all_to_all x1, waiting for transfers between devices, body(): lax.all_to_all(found_keys, 'wa', split_axis=0, concat_axis=0, tiled=True)  155 us
    all_to_all x1, waiting for transfers between devices, body(): lax.all_to_all(found_vals, 'wa', split_axis=0, concat_axis=0, tiled=True)  125 us
    all_to_all x1, starting transfers between devices, body(): lax.all_to_all(found_vals, 'wa', split_axis=0, concat_axis=0, tiled=True)  89.1 us
    ppermute x2, waiting for transfers between devices, with_halo(): before = lax.ppermute(last, axis, up)  87.5 us
    dot_general x6, matrix products, one_group(): jnp.einsum('gqk,kgd->qgd', rounded, val_part, preferred_element_type=jnp....  79.9 us
    reduce_sum x6, other arithmetic, one_group(): totals = jnp.sum(weights, axis=-1)  74.7 us
    dynamic_slice x12, local copies, waits for them, and re-layouts, one_group(): lax.dynamic_slice_in_dim(all_vals, begin, span, 1)  68.2 us
    dot_general x6, matrix products, one_group(): jnp.einsum('qgd,kgd->gqk', query_part, key_part, preferred_element_type=j...  67.8 us
  transfers between devices with their start and end apart: 6, of which 4 were waited for; matrix products, arithmetic and copies ran while one was open for 6% of the time, Pallas kernels for 0%

commit v1 on v0

v1 whole, which is shorter than its diff:
```python
import functools
import math

import jax
import jax.numpy as jnp
from jax import lax
from jax.experimental import pallas as pl
from jax.experimental.pallas import tpu as pltpu
from jax.sharding import PartitionSpec as P

HEAD = 128
CUBE = 32
LOG_SCALE = HEAD ** -0.5 * math.log2(math.e)
NEG = -1e30
VMEM = 56 << 20


def dot_t(a, b):
    return lax.dot_general(a, b, (((1,), (1,)), ((), ())), preferred_element_type=jnp.float32)


def dot(a, b):
    return lax.dot_general(a, b, (((1,), (0,)), ((), ())), preferred_element_type=jnp.float32)


def partial_softmax(scores, vals):
    top = functools.reduce(jnp.maximum, [jnp.max(s, axis=1, keepdims=True) for s in scores])
    total = 0.0
    mixed = 0.0
    for s, v in zip(scores, vals):
        w = jnp.exp2((s - top) * LOG_SCALE)
        total = total + jnp.sum(w, axis=1, keepdims=True)
        mixed = mixed + dot(w.astype(jnp.bfloat16), v)
    return mixed / total, top * LOG_SCALE + jnp.log2(total)


def window_kernel(place, q, qu, qd, kl, kc, kr, vl, vc, vr, o, ou, od, lo, lu, ld):
    head = pl.program_id(0)
    lane = lax.broadcasted_iota(jnp.int32, (q.shape[1], HEAD), 1)
    keys = (kl, kc, kr)
    vals = (vl, vc, vr)

    def run(cols):
        for query, out, lse, rows in (
            (qu, ou, lu, (0,)),
            (qd, od, ld, (1,)),
            (q.at[0], o.at[0], lo.at[0], (0, 1)),
            (q.at[1], o.at[1], lo.at[1], (0, 1)),
        ):
            picks = [(c, r) for c in cols for r in rows]
            scores = [dot_t(query[...], keys[c][r]) for c, r in picks]
            mixed, level = partial_softmax(scores, [vals[c][r] for c, r in picks])
            out[...] = mixed.astype(out.dtype)
            lse[...] = jnp.where(lane == head, level, lse[...])

    first = place[0] == 0
    last = place[0] == place[1] - 1

    @pl.when(jnp.logical_not(first | last))
    def _():
        run((0, 1, 2))

    @pl.when(first)
    def _():
        run((1, 2))

    @pl.when(last)
    def _():
        run((0, 1))


def window(place, q, qu, qd, kl, kc, kr, vl, vc, vr):
    rows, tile, feat = q.shape
    heads = feat // HEAD
    two = pl.BlockSpec((rows, tile, HEAD), lambda h, *_: (0, 0, h))
    one = pl.BlockSpec((tile, HEAD), lambda h, *_: (0, h))
    two_c = pl.BlockSpec((rows, tile, HEAD), lambda h, *_: (0, 0, 0))
    one_c = pl.BlockSpec((tile, HEAD), lambda h, *_: (0, 0))
    f32 = jnp.float32
    shape = jax.ShapeDtypeStruct
    return pl.pallas_call(
        window_kernel,
        grid_spec=pltpu.PrefetchScalarGridSpec(
            num_scalar_prefetch=1,
            grid=(heads,),
            in_specs=[two, one, one] + [two] * 6,
            out_specs=[two, one, one, two_c, one_c, one_c],
        ),
        out_shape=[
            shape((rows, tile, feat), f32),
            shape((tile, feat), jnp.bfloat16),
            shape((tile, feat), jnp.bfloat16),
            shape((rows, tile, HEAD), f32),
            shape((tile, HEAD), f32),
            shape((tile, HEAD), f32),
        ],
        compiler_params=pltpu.CompilerParams(vmem_limit_bytes=VMEM),
        cost_estimate=pl.CostEstimate(
            flops=4 * rows * tile * 9 * tile * feat, bytes_accessed=30 << 20, transcendentals=rows * tile * 9 * tile * heads
        ),
        name="window",
    )(place, q, qu, qd, kl, kc, kr, vl, vc, vr)


def cube_kernel(spots, counts, has, q, ck, cv, o, lo, ou, od, lu, ld, out, kbuf, vbuf):
    head = pl.program_id(0)
    tile = q.shape[1]
    slots = spots.shape[1]
    lane = lax.broadcasted_iota(jnp.int32, (tile, HEAD), 1)

    def column(x):
        return jnp.sum(jnp.where(lane == head, x, 0.0), axis=1, keepdims=True)

    for t, (ext, lext) in enumerate(((od, ld), (ou, lu))):
        for s in range(slots):
            spot = spots[t, s]
            kbuf[t, s * CUBE : (s + 1) * CUBE, :] = ck[spot // 2, spot % 2]
            vbuf[t, s * CUBE : (s + 1) * CUBE, :] = cv[spot // 2, spot % 2]
        slot = lax.broadcasted_iota(jnp.int32, (1, slots * CUBE), 1) // CUBE
        scores = jnp.where(slot < counts[t], dot_t(q[t], kbuf[t]), NEG)
        mixed, level = partial_softmax([scores], [vbuf[t]])
        win_level = column(lo[t])
        ext_level = jnp.where(has[t] > 0, column(lext[...]), NEG)
        top = jnp.maximum(jnp.maximum(level, win_level), ext_level)
        a = jnp.exp2(level - top)
        b = jnp.exp2(win_level - top)
        c = jnp.exp2(ext_level - top)
        total = a + b + c
        out[t] = ((mixed * a + o[t] * b + ext[...].astype(jnp.float32) * c) / total).astype(out.dtype)


def cubes(spots, counts, has, q, fetched, o, lo, ou, od, lu, ld):
    rows, tile, feat = q.shape
    heads = feat // HEAD
    cols = fetched.shape[0]
    slots = spots.shape[1]
    two = pl.BlockSpec((rows, tile, HEAD), lambda h, *_: (0, 0, h))
    one = pl.BlockSpec((tile, HEAD), lambda h, *_: (0, h))
    two_c = pl.BlockSpec((rows, tile, HEAD), lambda h, *_: (0, 0, 0))
    one_c = pl.BlockSpec((tile, HEAD), lambda h, *_: (0, 0))
    ck = pl.BlockSpec((cols, None, 2, CUBE, HEAD), lambda h, *_: (0, 0, 0, 0, h))
    cv = pl.BlockSpec((cols, None, 2, CUBE, HEAD), lambda h, *_: (0, 1, 0, 0, h))
    return pl.pallas_call(
        cube_kernel,
        grid_spec=pltpu.PrefetchScalarGridSpec(
            num_scalar_prefetch=3,
            grid=(heads,),
            in_specs=[two, ck, cv, two, two_c, one, one, one_c, one_c],
            out_specs=two,
            scratch_shapes=[pltpu.VMEM((rows, slots * CUBE, HEAD), jnp.bfloat16)] * 2,
        ),
        out_shape=jax.ShapeDtypeStruct((rows, tile, feat), jnp.bfloat16),
        compiler_params=pltpu.CompilerParams(vmem_limit_bytes=VMEM),
        cost_estimate=pl.CostEstimate(
            flops=4 * rows * tile * slots * CUBE * feat, bytes_accessed=20 << 20, transcendentals=rows * tile * slots * CUBE * heads
        ),
        name="cubes",
    )(spots, counts, has, q, fetched, fetched, o, lo, ou, od, lu, ld)


def body(queries, keys, values, selected, counts):
    rows = queries.shape[0]
    tile = queries.shape[2]
    feat = queries.shape[3]
    slots = selected.shape[2]
    columns = lax.axis_size("wa")
    bands = lax.axis_size("ha")
    cubes_dev = rows * (tile // CUBE)
    q, k, v = (x[:, 0] for x in (queries, keys, values))
    right = [(i, i + 1) for i in range(columns - 1)]
    left = [(i + 1, i) for i in range(columns - 1)]
    down = [(i, i + 1) for i in range(bands - 1)]
    up = [(i + 1, i) for i in range(bands - 1)]

    kl, kr = lax.ppermute(k, "wa", right), lax.ppermute(k, "wa", left)
    vl, vr = lax.ppermute(v, "wa", right), lax.ppermute(v, "wa", left)
    qu, qd = lax.ppermute(q[1], "ha", down), lax.ppermute(q[0], "ha", up)

    ids = selected.reshape(rows * slots)
    owner = ids // cubes_dev
    local = ids % cubes_dev
    same = owner[:, None] == owner[None, :]
    before = jnp.arange(rows * slots)[:, None] > jnp.arange(rows * slots)[None, :]
    rank = jnp.sum((same & before).astype(jnp.int32), axis=1)
    spots = owner * 2 + rank
    place_at = spots[:, None] == jnp.arange(columns * 2, dtype=jnp.int32)[None, :]
    requests = jnp.sum(jnp.where(place_at, local[:, None], 0), axis=0).reshape(columns, 2)
    asked = lax.all_to_all(requests, "wa", split_axis=0, concat_axis=0, tiled=True)
    ktab = k.reshape(cubes_dev, CUBE, feat)
    vtab = v.reshape(cubes_dev, CUBE, feat)
    found = jnp.stack([ktab[asked], vtab[asked]], axis=1)
    fetched = lax.all_to_all(found, "wa", split_axis=0, concat_axis=0, tiled=True)

    row = lax.axis_index("ha")
    col = lax.axis_index("wa")
    place = jnp.stack([col, jnp.int32(columns)]).astype(jnp.int32)
    has = jnp.stack([row > 0, row < bands - 1]).astype(jnp.int32)
    o, ou, od, lo, lu, ld = window(place, q, qu, qd, kl, k, kr, vl, v, vr)
    ou, lu = lax.ppermute(ou, "ha", up), lax.ppermute(lu, "ha", up)
    od, ld = lax.ppermute(od, "ha", down), lax.ppermute(ld, "ha", down)
    out = cubes(spots.reshape(rows, slots), counts[:, 0], has, q, fetched, o, lo, ou, od, lu, ld)
    return out[:, None]


def solution(mesh):
    return jax.shard_map(
        body,
        mesh=mesh,
        in_specs=(
            P("ha", "wa", None, None),
            P("ha", "wa", None, None),
            P("ha", "wa", None, None),
            P("ha", "wa", None),
            P("ha", "wa"),
        ),
        out_specs=P("ha", "wa", None, None),
        check_vma=False,
    )
```

time: 1040 us -> 448 us (0.43)
  the two profiles are of different devices: /device:TPU:7 before, /device:TPU:26 now
where the time goes in v1:
time: 448 us
  waiting for transfers between devices  282 us (63%)
  Pallas kernels  82.6 us (18%)
  starting transfers between devices  37.9 us (8%)
  blocking collectives  15.4 us (3%)
  local copies, waits for them, and re-layouts  15 us (3%)
  other arithmetic  14.8 us (3%)
    ppermute x2, waiting for transfers between devices, body(): qu, qd = (lax.ppermute(q[1], 'ha', down), lax.ppermute(q[0], 'ha', up))  136 us
    ppermute x2, waiting for transfers between devices, body(): kl, kr = (lax.ppermute(k, 'wa', right), lax.ppermute(k, 'wa', left))  87.3 us
    pallas_call x1, Pallas kernels, window(): pl.pallas_call(window_kernel, grid_spec=pltpu.PrefetchScalarGridSpec(num_...  56 us
    ppermute x2, waiting for transfers between devices, body(): vl, vr = (lax.ppermute(v, 'wa', right), lax.ppermute(v, 'wa', left))  48 us
    pallas_call x1, Pallas kernels, cubes(): pl.pallas_call(cube_kernel, grid_spec=pltpu.PrefetchScalarGridSpec(num_sc...  26.6 us
    all_to_all x1, blocking collectives, body(): lax.all_to_all(requests, 'wa', split_axis=0, concat_axis=0, tiled=True)  15.4 us
    another operation x1, other arithmetic, body(): found = jnp.stack([ktab[asked], vtab[asked]], axis=1)  10.6 us
    gather x2, local copies, waits for them, and re-layouts, body(): found = jnp.stack([ktab[asked], vtab[asked]], axis=1)  10.4 us
  transfers between devices with their start and end apart: 11, of which 6 were waited for; matrix products, arithmetic and copies ran while one was open for 1% of the time, Pallas kernels for 13%

profile of v1, /device:TPU:26, one launch (start us, length us, event | category | flops | bytes accessed | tf_op | source)
XLA Modules:
  0.0 447.8 jit_solution(13799221499629422754)
XLA Ops:
  3.2 15.4 %all_to_all.17 = s32[32,1,2]{2,1,0:T(1,128)S(1)} all-to-all(s32[32,1,2]{2,1,0:T(1,128)S(1)} %bitcast.38), channel_id=1, replica_groups=mesh['ha'=4,'wa'=32] {'wa'}, dimensions={0} | all-to-all | bytes 512 | tf_op jit(solution)/shard_map/all_to_all | solution.py:188
  18.9 5.2 %gather_fusion.1 = bf16[64,32,1536]{2,1,0:T(8,128)(2,1)} fusion(bf16[24,32,1536]{2,1,0:T(8,128)(2,1)} %bitcast.32, s32[1024]{0:T(1024)S(1)} %pad_clamp_fusion), kind=kCustom, calls=%fused_computation.1 | custom fusion | bytes 12583168 | tf_op jit(solution)/shard_map/gather | solution.py:191
  24.1 5.2 %gather_fusion = bf16[64,32,1536]{2,1,0:T(8,128)(2,1)} fusion(bf16[24,32,1536]{2,1,0:T(8,128)(2,1)} %bitcast.5, s32[1024]{0:T(1024)S(1)} %pad_clamp_fusion), kind=kCustom, calls=%fused_computation | custom fusion | bytes 12583168 | tf_op jit(solution)/shard_map/gather | solution.py:191
  29.3 10.6 %pad_maximum_fusion = bf16[32,2,2,32,1536]{4,3,2,1,0:T(8,128)(2,1)} fusion(bf16[32,1,2,32,1536]{4,3,2,1,0:T(8,128)(2,1)} %bitcast.30, bf16[32,1,2,32,1536]{4,3,2,1,0:T(8,128)(2,1)} %bitcast.31), kind=kLoop, calls=%fused_computation.2 | loop fusion | flops 6291456 | bytes 25165824 | tf_op jit(solution)/shard_map/stack | solution.py:191
  40.0 7.1 %all-to-all-start.1 = ((bf16[32,2,2,32,1536]{4,3,2,1,0:T(8,128)(2,1)}), bf16[32,2,2,32,1536]{4,3,2,1,0:T(8,128)(2,1)}, u32[]{:S(2)}, u32[]{:S(2)}) async-start(bf16[32,2,2,32,1536]{4,3,2,1,0:T(8,128)(2,1)} %pad_maximum_fusion), calls=%async_computation.1 | async-start | bytes 25165824 | tf_op jit(solution)/shard_map/all_to_all | solution.py:192
  47.1 1.9 slice_bitcast_fusion
  49.0 1.9 collective-permute-start
  50.9 3.4 collective-permute-start.2
  54.3 4.6 %collective-permute-start.3 = (bf16[2,384,1536]{2,1,0:T(8,128)(2,1)}, bf16[2,384,1536]{2,1,0:T(8,128)(2,1)}, u32[]{:S(2)}, u32[]{:S(2)}) collective-permute-start(bf16[2,384,1536]{2,1,0:T(8,128)(2,1)} %bitcast.14.kc), channel_id=1, source_target_pairs={{1,0},{2,1},{3,2},{4,3},{5,4},{6,5},{7,6},{8,7},{9,8},{10,9},{11,1... | collective-permute-start | bytes 7077896 | tf_op jit(solution)/shard_map/ppermute | solution.py:175
  58.9 1.9 collective-permute-start.4
  60.9 6.0 %collective-permute-start.5 = (bf16[2,384,1536]{2,1,0:T(8,128)(2,1)S(1)}, bf16[2,384,1536]{2,1,0:T(8,128)(2,1)}, u32[]{:S(2)}, u32[]{:S(2)}) collective-permute-start(bf16[2,384,1536]{2,1,0:T(8,128)(2,1)S(1)} %bitcast.35), channel_id=1, source_target_pairs={{1,0},{2,1},{3,2},{4,3},{5,4},{6,5},{7,6},{8,7},{9,8},{10,9},{11,1... | collective-permute-start | bytes 7077896 | tf_op jit(solution)/shard_map/ppermute | solution.py:176
  66.9 107.5 %collective-permute-done.qu = bf16[384,1536]{1,0:T(8,128)(2,1)S(1)} collective-permute-done((bf16[384,1536]{1,0:T(8,128)(2,1)S(1)}, bf16[384,1536]{1,0:T(8,128)(2,1)S(1)}, u32[]{:S(2)}, u32[]{:S(2)}) %collective-permute-start) | collective-permute-done | bytes 1179680 | tf_op jit(solution)/shard_map/ppermute | solution.py:177
  174.4 2.1 collective-permute-start.1
  177.1 28.1 %collective-permute-done.1.qd = bf16[384,1536]{1,0:T(8,128)(2,1)} collective-permute-done((bf16[384,1536]{1,0:T(8,128)(2,1)S(1)}, bf16[384,1536]{1,0:T(8,128)(2,1)}, u32[]{:S(2)}, u32[]{:S(2)}) %collective-permute-start.1) | collective-permute-done | bytes 1179680 | tf_op jit(solution)/shard_map/ppermute | solution.py:177
  205.2 87.3 %collective-permute-done.2.kl = bf16[2,384,1536]{2,1,0:T(8,128)(2,1)} collective-permute-done((bf16[2,384,1536]{2,1,0:T(8,128)(2,1)}, bf16[2,384,1536]{2,1,0:T(8,128)(2,1)}, u32[]{:S(2)}, u32[]{:S(2)}) %collective-permute-start.2) | collective-permute-done | bytes 2359328 | tf_op jit(solution)/shard_map/ppermute | solution.py:175
  292.5 48.0 %collective-permute-done.4.vl = bf16[2,384,1536]{2,1,0:T(8,128)(2,1)} collective-permute-done((bf16[2,384,1536]{2,1,0:T(8,128)(2,1)S(1)}, bf16[2,384,1536]{2,1,0:T(8,128)(2,1)}, u32[]{:S(2)}, u32[]{:S(2)}) %collective-permute-start.4) | collective-permute-done | bytes 2359328 | tf_op jit(solution)/shard_map/ppermute | solution.py:176
  340.4 56.0 %window.1 = (f32[2,384,1536]{2,1,0:T(8,128)}, bf16[384,1536]{1,0:T(8,128)(2,1)}, bf16[384,1536]{1,0:T(8,128)(2,1)}, f32[2,384,128]{2,1,0:T(8,128)}, f32[384,128]{1,0:T(8,128)}, /*index=5*/f32[384,128]{1,0:T(8,128)}) custom-call(s32[2]{0:T(128)} %pad_add_fusion.place, bf16[2,384,1536]{2,1,0:T(8,128)(2,1)} %bitcast.36, bf16[384,1536]{1,0:T(8,128)(2,1)} %copy-done.5, ...), custom_call_target="tpu_custom_call" | custom-call | flops 16307453952 | bytes 31457280 | tf_op jit(solution)/shard_map/window/pallas_call | solution.py:81
  396.4 1.9 collective-permute-start.6
  398.4 2.5 collective-permute-start.7
  401.6 4.6 %collective-permute-start.8 = (f32[384,128]{1,0:T(8,128)}, f32[384,128]{1,0:T(8,128)S(1)}, u32[]{:S(2)}, u32[]{:S(2)}) collective-permute-start(f32[384,128]{1,0:T(8,128)} %get-tuple-element.15), channel_id=1, source_target_pairs={{32,0},{64,32},{96,64},{33,1},{65,33},{97,65},{34,2},{66,34},{98,6... | collective-permute-start | bytes 589832 | tf_op jit(solution)/shard_map/ppermute | solution.py:199
  406.2 1.9 collective-permute-start.9
  408.7 5.8 %collective-permute-done.8.lu = f32[384,128]{1,0:T(8,128)S(1)} collective-permute-done((f32[384,128]{1,0:T(8,128)}, f32[384,128]{1,0:T(8,128)S(1)}, u32[]{:S(2)}, u32[]{:S(2)}) %collective-permute-start.8) | collective-permute-done | bytes 196640 | tf_op jit(solution)/shard_map/ppermute | solution.py:199
  414.5 5.2 %collective-permute-done.9.ld = f32[384,128]{1,0:T(8,128)S(1)} collective-permute-done((f32[384,128]{1,0:T(8,128)}, f32[384,128]{1,0:T(8,128)S(1)}, u32[]{:S(2)}, u32[]{:S(2)}) %collective-permute-start.9) | collective-permute-done | bytes 196640 | tf_op jit(solution)/shard_map/ppermute | solution.py:200
  421.2 26.6 %cubes.1 = bf16[2,384,1536]{2,1,0:T(8,128)(2,1)} custom-call(s32[2,32]{1,0:T(2,128)} %fusion.2.spots, s32[2]{0:T(128)} %bitcast.40, s32[2]{0:T(128)} %add_convert_fusion.has, bf16[2,384,1536]{2,1,0:T(8,128)(2,1)} %bitcast.37, bf16[32,2,2,32,1536]{4,3,2,1,0:T(8,128)(2,1)} %all-to-all-done.1.ck.cv, bf16[32,2,2,32,1536]{4,3,2,1,0:T(8,128)(2,1)} %all-to-all-done.1.ck.cv, ...), custom_call_target="tpu_custom_call" | custom-call | flops 4831838208 | bytes 20971520 | tf_op jit(solution)/shard_map/cubes/pallas_call | solution.py:143
  (37 shorter events, 6.8 us)
Async XLA Ops:
  40.0 379.8 %all-to-all-start.1 = ((bf16[32,2,2,32,1536]{4,3,2,1,0:T(8,128)(2,1)}), bf16[32,2,2,32,1536]{4,3,2,1,0:T(8,128)(2,1)}, u32[]{:S(2)}, u32[]{:S(2)}) async-start(bf16[32,2,2,32,1536]{4,3,2,1,0:T(8,128)(2,1)} %pad_maximum_fusion), calls=%async_computation.1 | async-start | bytes 25165824 | tf_op jit(solution)/shard_map/all_to_all | solution.py:192
  47.1 11.9 %copy-start = (bf16[2,1,384,1536]{3,2,1,0:T(8,128)(2,1)S(1)}, bf16[2,1,384,1536]{3,2,1,0:T(8,128)(2,1)}, u32[]{:S(2)}) copy-start(bf16[2,1,384,1536]{3,2,1,0:T(8,128)(2,1)} %param.7) | copy-start | bytes 7077892
  49.0 125.4 %collective-permute-start = (bf16[384,1536]{1,0:T(8,128)(2,1)S(1)}, bf16[384,1536]{1,0:T(8,128)(2,1)S(1)}, u32[]{:S(2)}, u32[]{:S(2)}) collective-permute-start(bf16[384,1536]{1,0:T(8,128)(2,1)S(1)} %get-tuple-element.20), channel_id=1, source_target_pairs={{0,32},{32,64},{64,96},{1,33},{33,65},{65,97},{2,34},{34,66},{66,9... | collective-permute-start | bytes 3538952 | tf_op jit(solution)/shard_map/ppermute | solution.py:177
  50.9 241.5 %collective-permute-start.2 = (bf16[2,384,1536]{2,1,0:T(8,128)(2,1)}, bf16[2,384,1536]{2,1,0:T(8,128)(2,1)}, u32[]{:S(2)}, u32[]{:S(2)}) collective-permute-start(bf16[2,384,1536]{2,1,0:T(8,128)(2,1)} %bitcast.14.kc), channel_id=1, source_target_pairs={{0,1},{1,2},{2,3},{3,4},{4,5},{5,6},{6,7},{7,8},{8,9},{9,10},{10,1... | collective-permute-start | bytes 7077896 | tf_op jit(solution)/shard_map/ppermute | solution.py:175
  54.3 238.1 %collective-permute-start.3 = (bf16[2,384,1536]{2,1,0:T(8,128)(2,1)}, bf16[2,384,1536]{2,1,0:T(8,128)(2,1)}, u32[]{:S(2)}, u32[]{:S(2)}) collective-permute-start(bf16[2,384,1536]{2,1,0:T(8,128)(2,1)} %bitcast.14.kc), channel_id=1, source_target_pairs={{1,0},{2,1},{3,2},{4,3},{5,4},{6,5},{7,6},{8,7},{9,8},{10,9},{11,1... | collective-permute-start | bytes 7077896 | tf_op jit(solution)/shard_map/ppermute | solution.py:175
  58.9 281.5 %collective-permute-start.4 = (bf16[2,384,1536]{2,1,0:T(8,128)(2,1)S(1)}, bf16[2,384,1536]{2,1,0:T(8,128)(2,1)}, u32[]{:S(2)}, u32[]{:S(2)}) collective-permute-start(bf16[2,384,1536]{2,1,0:T(8,128)(2,1)S(1)} %bitcast.34), channel_id=1, source_target_pairs={{0,1},{1,2},{2,3},{3,4},{4,5},{5,6},{6,7},{7,8},{8,9},{9,10},{10,1... | collective-permute-start | bytes 7077896 | tf_op jit(solution)/shard_map/ppermute | solution.py:176
  60.9 279.6 %collective-permute-start.5 = (bf16[2,384,1536]{2,1,0:T(8,128)(2,1)S(1)}, bf16[2,384,1536]{2,1,0:T(8,128)(2,1)}, u32[]{:S(2)}, u32[]{:S(2)}) collective-permute-start(bf16[2,384,1536]{2,1,0:T(8,128)(2,1)S(1)} %bitcast.35), channel_id=1, source_target_pairs={{1,0},{2,1},{3,2},{4,3},{5,4},{6,5},{7,6},{8,7},{9,8},{10,9},{11,1... | collective-permute-start | bytes 7077896 | tf_op jit(solution)/shard_map/ppermute | solution.py:176
  174.4 2.1 copy-start.5
  174.4 30.7 %collective-permute-start.1 = (bf16[384,1536]{1,0:T(8,128)(2,1)S(1)}, bf16[384,1536]{1,0:T(8,128)(2,1)}, u32[]{:S(2)}, u32[]{:S(2)}) collective-permute-start(bf16[384,1536]{1,0:T(8,128)(2,1)S(1)} %get-tuple-element.19), channel_id=1, source_target_pairs={{32,0},{64,32},{96,64},{33,1},{65,33},{97,65},{34,2},{66,34},{98,6... | collective-permute-start | bytes 3538952 | tf_op jit(solution)/shard_map/ppermute | solution.py:177
  396.4 23.3 %collective-permute-start.6 = (bf16[384,1536]{1,0:T(8,128)(2,1)}, bf16[384,1536]{1,0:T(8,128)(2,1)S(1)}, u32[]{:S(2)}, u32[]{:S(2)}) collective-permute-start(bf16[384,1536]{1,0:T(8,128)(2,1)} %get-tuple-element.13), channel_id=1, source_target_pairs={{32,0},{64,32},{96,64},{33,1},{65,33},{97,65},{34,2},{66,34},{98,6... | collective-permute-start | bytes 3538952 | tf_op jit(solution)/shard_map/ppermute | solution.py:199
  398.4 21.4 %collective-permute-start.7 = (bf16[384,1536]{1,0:T(8,128)(2,1)}, bf16[384,1536]{1,0:T(8,128)(2,1)S(1)}, u32[]{:S(2)}, u32[]{:S(2)}) collective-permute-start(bf16[384,1536]{1,0:T(8,128)(2,1)} %get-tuple-element.14), channel_id=1, source_target_pairs={{0,32},{32,64},{64,96},{1,33},{33,65},{65,97},{2,34},{34,66},{66,9... | collective-permute-start | bytes 3538952 | tf_op jit(solution)/shard_map/ppermute | solution.py:200
  401.6 12.9 %collective-permute-start.8 = (f32[384,128]{1,0:T(8,128)}, f32[384,128]{1,0:T(8,128)S(1)}, u32[]{:S(2)}, u32[]{:S(2)}) collective-permute-start(f32[384,128]{1,0:T(8,128)} %get-tuple-element.15), channel_id=1, source_target_pairs={{32,0},{64,32},{96,64},{33,1},{65,33},{97,65},{34,2},{66,34},{98,6... | collective-permute-start | bytes 589832 | tf_op jit(solution)/shard_map/ppermute | solution.py:199
  406.2 13.5 %collective-permute-start.9 = (f32[384,128]{1,0:T(8,128)}, f32[384,128]{1,0:T(8,128)S(1)}, u32[]{:S(2)}, u32[]{:S(2)}) collective-permute-start(f32[384,128]{1,0:T(8,128)} %get-tuple-element.16), channel_id=1, source_target_pairs={{0,32},{32,64},{64,96},{1,33},{33,65},{65,97},{2,34},{34,66},{66,9... | collective-permute-start | bytes 589832 | tf_op jit(solution)/shard_map/ppermute | solution.py:200
  414.5 5.3 %copy-start.3 = (f32[384,128]{1,0:T(8,128)}, f32[384,128]{1,0:T(8,128)S(1)}, u32[]{:S(2)}) copy-start(f32[384,128]{1,0:T(8,128)S(1)} %collective-permute-done.8.lu) | copy-start | bytes 589828
  419.7 0.7 copy-start.4
  419.7 1.1 copy-start.1
  419.7 1.4 copy-start.2

commit v2 on v1

--- a/solution.py
+++ b/solution.py
@@ -10,6 +10,7 @@
 
 HEAD = 128
 CUBE = 32
+DEPTH = 4
 LOG_SCALE = HEAD ** -0.5 * math.log2(math.e)
 NEG = -1e30
 VMEM = 56 << 20
@@ -102,23 +103,29 @@
     )(place, q, qu, qd, kl, kc, kr, vl, vc, vr)
 
 
-def cube_kernel(spots, counts, has, q, ck, cv, o, lo, ou, od, lu, ld, out, kbuf, vbuf):
+def cube_kernel(slot_of, counts, has, q, *refs):
+    sources, (o, lo, ou, od, lu, ld, out, kbuf, vbuf) = refs[:6], refs[6:]
     head = pl.program_id(0)
-    tile = q.shape[1]
-    slots = spots.shape[1]
+    rows, tile = q.shape[0], q.shape[1]
     lane = lax.broadcasted_iota(jnp.int32, (tile, HEAD), 1)
 
     def column(x):
         return jnp.sum(jnp.where(lane == head, x, 0.0), axis=1, keepdims=True)
 
+    index = 0
+    for ck, cv in (sources[0:2], sources[2:4], sources[4:6]):
+        for at in range(ck.shape[0]):
+            for rank in range(2):
+                spot = pl.ds(pl.multiple_of(slot_of[index] * CUBE, CUBE), CUBE)
+                kbuf[spot, :] = ck[at, rank]
+                vbuf[spot, :] = cv[at, rank]
+                index += 1
+    span = index * CUBE // rows
     for t, (ext, lext) in enumerate(((od, ld), (ou, lu))):
-        for s in range(slots):
-            spot = spots[t, s]
-            kbuf[t, s * CUBE : (s + 1) * CUBE, :] = ck[spot // 2, spot % 2]
-            vbuf[t, s * CUBE : (s + 1) * CUBE, :] = cv[spot // 2, spot % 2]
-        slot = lax.broadcasted_iota(jnp.int32, (1, slots * CUBE), 1) // CUBE
-        scores = jnp.where(slot < counts[t], dot_t(q[t], kbuf[t]), NEG)
-        mixed, level = partial_softmax([scores], [vbuf[t]])
+        part = pl.ds(t * span, span)
+        slot = lax.broadcasted_iota(jnp.int32, (1, span), 1) // CUBE
+        scores = jnp.where(slot < counts[t], dot_t(q[t], kbuf[part, :]), NEG)
+        mixed, level = partial_softmax([scores], [vbuf[part, :]])
         win_level = column(lo[t])
         ext_level = jnp.where(has[t] > 0, column(lext[...]), NEG)
         top = jnp.maximum(jnp.maximum(level, win_level), ext_level)
@@ -129,33 +136,88 @@
         out[t] = ((mixed * a + o[t] * b + ext[...].astype(jnp.float32) * c) / total).astype(out.dtype)
 
 
-def cubes(spots, counts, has, q, fetched, o, lo, ou, od, lu, ld):
+def cubes(slot_of, counts, has, q, own, near, far, o, lo, ou, od, lu, ld):
     rows, tile, feat = q.shape
     heads = feat // HEAD
-    cols = fetched.shape[0]
-    slots = spots.shape[1]
+    keys = slot_of.shape[0] * CUBE
     two = pl.BlockSpec((rows, tile, HEAD), lambda h, *_: (0, 0, h))
     one = pl.BlockSpec((tile, HEAD), lambda h, *_: (0, h))
     two_c = pl.BlockSpec((rows, tile, HEAD), lambda h, *_: (0, 0, 0))
     one_c = pl.BlockSpec((tile, HEAD), lambda h, *_: (0, 0))
-    ck = pl.BlockSpec((cols, None, 2, CUBE, HEAD), lambda h, *_: (0, 0, 0, 0, h))
-    cv = pl.BlockSpec((cols, None, 2, CUBE, HEAD), lambda h, *_: (0, 1, 0, 0, h))
+
+    def block(x, kv):
+        if x.ndim == 6:
+            return pl.BlockSpec((x.shape[0], None, None, 2, CUBE, HEAD), lambda h, *_: (0, 0, kv, 0, 0, h))
+        return pl.BlockSpec((x.shape[0], None, 2, CUBE, HEAD), lambda h, *_: (0, kv, 0, 0, h))
+
+    near = near.reshape((-1,) + near.shape[2:])
     return pl.pallas_call(
         cube_kernel,
         grid_spec=pltpu.PrefetchScalarGridSpec(
             num_scalar_prefetch=3,
             grid=(heads,),
-            in_specs=[two, ck, cv, two, two_c, one, one, one_c, one_c],
+            in_specs=[two]
+            + [block(x, kv) for x in (own, near, far) for kv in range(2)]
+            + [two, two_c, one, one, one_c, one_c],
             out_specs=two,
-            scratch_shapes=[pltpu.VMEM((rows, slots * CUBE, HEAD), jnp.bfloat16)] * 2,
+            scratch_shapes=[pltpu.VMEM((keys, HEAD), jnp.bfloat16)] * 2,
         ),
         out_shape=jax.ShapeDtypeStruct((rows, tile, feat), jnp.bfloat16),
         compiler_params=pltpu.CompilerParams(vmem_limit_bytes=VMEM),
         cost_estimate=pl.CostEstimate(
-            flops=4 * rows * tile * slots * CUBE * feat, bytes_accessed=20 << 20, transcendentals=rows * tile * slots * CUBE * heads
+            flops=4 * tile * keys * feat, bytes_accessed=20 << 20, transcendentals=tile * keys * heads
         ),
         name="cubes",
-    )(spots, counts, has, q, fetched, fetched, o, lo, ou, od, lu, ld)
+    )(slot_of, counts, has, q, own, own, near, near, far, far, o, lo, ou, od, lu, ld)
+
+
+def pick_kernel(ids, *refs):
+    tables, (out, held, into, back) = refs[:-4], refs[-4:]
+    groups, sides, kinds, ranks = out.shape[:4]
+    pairs = []
+    for g in range(groups):
+        for s in range(sides):
+            for kv in range(kinds):
+                table = tables[kv if len(tables) == kinds else s * kinds + kv]
+                for r in range(ranks):
+                    at = len(pairs)
+                    pairs.append(
+                        (
+                            pltpu.make_async_copy(table.at[ids[g, s, r]], held.at[at], into.at[at]),
+                            pltpu.make_async_copy(held.at[at], out.at[g, s, kv, r], back.at[at]),
+                        )
+                    )
+    for read, _ in pairs:
+        read.start()
+    for read, write in pairs:
+        read.wait()
+        write.start()
+    for _, write in pairs:
+        write.wait()
+
+
+def pick(ids, tables, name, weight):
+    feat = tables[0].shape[-1]
+    shape = ids.shape[:2] + (2,) + ids.shape[2:] + (CUBE, feat)
+    tables = [x.reshape(-1, CUBE, feat) for x in tables]
+    return pl.pallas_call(
+        pick_kernel,
+        grid_spec=pltpu.PrefetchScalarGridSpec(
+            num_scalar_prefetch=1,
+            grid=(1,),
+            in_specs=[pl.BlockSpec(memory_space=pl.ANY)] * len(tables),
+            out_specs=pl.BlockSpec(memory_space=pl.ANY),
+            scratch_shapes=[
+                pltpu.VMEM((math.prod(shape[:4]), CUBE, feat), tables[0].dtype),
+                pltpu.SemaphoreType.DMA((math.prod(shape[:4]),)),
+                pltpu.SemaphoreType.DMA((math.prod(shape[:4]),)),
+            ],
+        ),
+        out_shape=jax.ShapeDtypeStruct(shape, tables[0].dtype),
+        compiler_params=pltpu.CompilerParams(vmem_limit_bytes=VMEM),
+        cost_estimate=pl.CostEstimate(flops=0, bytes_accessed=weight * math.prod(shape), transcendentals=0),
+        name=name,
+    )(ids, *tables)
 
 
 def body(queries, keys, values, selected, counts):
@@ -167,14 +229,23 @@
     bands = lax.axis_size("ha")
     cubes_dev = rows * (tile // CUBE)
     q, k, v = (x[:, 0] for x in (queries, keys, values))
-    right = [(i, i + 1) for i in range(columns - 1)]
-    left = [(i + 1, i) for i in range(columns - 1)]
     down = [(i, i + 1) for i in range(bands - 1)]
     up = [(i + 1, i) for i in range(bands - 1)]
-
-    kl, kr = lax.ppermute(k, "wa", right), lax.ppermute(k, "wa", left)
-    vl, vr = lax.ppermute(v, "wa", right), lax.ppermute(v, "wa", left)
+    lines = columns // DEPTH
+    planes = [[line * DEPTH + z for line in range(lines)] for z in range(DEPTH)]
+    spin = [(i, i - i % DEPTH + (i + 1) % DEPTH) for i in range(columns)]
+    spun = [(j, i) for i, j in spin]
+    across = [(i, i - i % DEPTH + (i + 2) % DEPTH) for i in range(columns)]
+    ends = [(i, i + DEPTH) for i in range(0, columns - DEPTH, DEPTH)]
+    ends = ends + [(j + DEPTH - 1, i + DEPTH - 1) for i, j in ends]
+    steps = [(i, i + 1) for i in range(DEPTH - 1, columns - 1, DEPTH)]
+    steps = steps + [(j, i) for i, j in steps]
+    col = lax.axis_index("wa")
+    z = col % DEPTH
+
     qu, qd = lax.ppermute(q[1], "ha", down), lax.ppermute(q[0], "ha", up)
+    kl, kr = lax.ppermute(k, "wa", spin), lax.ppermute(k, "wa", spun)
+    vl, vr = lax.ppermute(v, "wa", spin), lax.ppermute(v, "wa", spun)
 
     ids = selected.reshape(rows * slots)
     owner = ids // cubes_dev
@@ -182,23 +253,44 @@
     same = owner[:, None] == owner[None, :]
     before = jnp.arange(rows * slots)[:, None] > jnp.arange(rows * slots)[None, :]
     rank = jnp.sum((same & before).astype(jnp.int32), axis=1)
-    spots = owner * 2 + rank
-    place_at = spots[:, None] == jnp.arange(columns * 2, dtype=jnp.int32)[None, :]
-    requests = jnp.sum(jnp.where(place_at, local[:, None], 0), axis=0).reshape(columns, 2)
-    asked = lax.all_to_all(requests, "wa", split_axis=0, concat_axis=0, tiled=True)
-    ktab = k.reshape(cubes_dev, CUBE, feat)
-    vtab = v.reshape(cubes_dev, CUBE, feat)
-    found = jnp.stack([ktab[asked], vtab[asked]], axis=1)
-    fetched = lax.all_to_all(found, "wa", split_axis=0, concat_axis=0, tiled=True)
+    place_at = (owner * 2 + rank)[:, None] == jnp.arange(columns * 2, dtype=jnp.int32)[None, :]
+    wanted = jnp.sum(jnp.where(place_at, local[:, None], 0), axis=0).reshape(columns, 2)
+    wanted = wanted.reshape(lines, DEPTH, 2)
+    wanted = jnp.stack([jnp.roll(wanted, 1, axis=1), wanted, jnp.roll(wanted, -1, axis=1)], axis=2)
+    wanted = wanted.reshape(columns, 3, 2)
+    asked = lax.all_to_all(wanted, "wa", split_axis=0, concat_axis=0, tiled=True)
+    asked = asked.reshape(lines, DEPTH, 3, 2)
+    asked_same = lax.dynamic_index_in_dim(asked, z, 1, keepdims=False)
+    asked_far = lax.dynamic_index_in_dim(asked, (z + 2) % DEPTH, 1, keepdims=False)
+    own = pick(jnp.stack([asked_same[:, 1], asked_far[:, 1]], axis=1), [k, v], "pick_own", 4)
+    own = lax.all_to_all(own, "wa", split_axis=0, concat_axis=0, tiled=True, axis_index_groups=planes)
+    far = lax.ppermute(own[:, 1], "wa", across)
+    kb = lax.ppermute(jnp.where(z == 0, kl, kr), "wa", ends)
+    vb = lax.ppermute(v, "wa", steps)
+    kl, kr, vl, vr, kb, vb, qu, qd = lax.optimization_barrier((kl, kr, vl, vr, kb, vb, qu, qd))
+    near = pick(jnp.stack([asked_same[:, 0], asked_same[:, 2]], axis=1), [kl, vl, kr, vr], "pick_near", 4)
+    near = lax.all_to_all(near, "wa", split_axis=0, concat_axis=0, tiled=True, axis_index_groups=planes)
+    kl, vl = jnp.where(z == 0, kb, kl), jnp.where(z == 0, vb, vl)
+    kr, vr = jnp.where(z == DEPTH - 1, kb, kr), jnp.where(z == DEPTH - 1, vb, vr)
+
+    ahead = (owner - z) % DEPTH
+    line = owner // DEPTH
+    spot = jnp.where(
+        ahead == 0,
+        line * 2,
+        jnp.where(ahead == 2, 6 * lines + line * 2, 2 * lines + line * 4 + jnp.where(ahead == 1, 2, 0)),
+    )
+    spot = spot + rank
+    entry = jnp.arange(rows * slots, dtype=jnp.int32)
+    slot_of = jnp.sum(jnp.where(spot[:, None] == entry[None, :], entry[:, None], 0), axis=0)
 
     row = lax.axis_index("ha")
-    col = lax.axis_index("wa")
     place = jnp.stack([col, jnp.int32(columns)]).astype(jnp.int32)
     has = jnp.stack([row > 0, row < bands - 1]).astype(jnp.int32)
     o, ou, od, lo, lu, ld = window(place, q, qu, qd, kl, k, kr, vl, v, vr)
     ou, lu = lax.ppermute(ou, "ha", up), lax.ppermute(lu, "ha", up)
     od, ld = lax.ppermute(od, "ha", down), lax.ppermute(ld, "ha", down)
-    out = cubes(spots.reshape(rows, slots), counts[:, 0], has, q, fetched, o, lo, ou, od, lu, ld)
+    out = cubes(slot_of, counts[:, 0], has, q, own, near, far, o, lo, ou, od, lu, ld)
     return out[:, None]
 
 

time: 448 us -> 328 us (0.73)
  the two profiles are of different devices: /device:TPU:26 before, /device:TPU:7 now
where the time goes in v2:
time: 328 us; the launch traced here: 324 us
  waiting for transfers between devices  142 us (43%)
  Pallas kernels  97.1 us (30%)
  starting transfers between devices  60.8 us (19%)
  other arithmetic  12.6 us (4%)
  local copies, waits for them, and re-layouts  11 us (3%)
    pallas_call x1, Pallas kernels, window(): pl.pallas_call(window_kernel, grid_spec=pltpu.PrefetchScalarGridSpec(num_...  56 us
    ppermute x2, waiting for transfers between devices, body(): vl, vr = (lax.ppermute(v, 'wa', spin), lax.ppermute(v, 'wa', spun))  46 us
    ppermute x2, waiting for transfers between devices, body(): kl, kr = (lax.ppermute(k, 'wa', spin), lax.ppermute(k, 'wa', spun))  42.4 us
    ppermute x2, waiting for transfers between devices, body(): qu, qd = (lax.ppermute(q[1], 'ha', down), lax.ppermute(q[0], 'ha', up))  37.4 us
    pallas_call x1, Pallas kernels, cubes(): pl.pallas_call(cube_kernel, grid_spec=pltpu.PrefetchScalarGridSpec(num_sc...  26.9 us
    pallas_call x2, Pallas kernels, pick(): pl.pallas_call(pick_kernel, grid_spec=pltpu.PrefetchScalarGridSpec(num_sc...  14.2 us
    ppermute x2, starting transfers between devices, body(): od, ld = (lax.ppermute(od, 'ha', down), lax.ppermute(ld, 'ha', down))  13.6 us
    ppermute x2, starting transfers between devices, body(): qu, qd = (lax.ppermute(q[1], 'ha', down), lax.ppermute(q[0], 'ha', up))  12.7 us
  transfers between devices with their start and end apart: 16, of which 6 were waited for; matrix products, arithmetic and copies ran while one was open for 5% of the time, Pallas kernels for 19%

profile of v2, /device:TPU:7, one launch (start us, length us, event | category | flops | bytes accessed | tf_op | source)
XLA Modules:
  0.0 324.2 jit_solution(16874353322543397523)
XLA Ops:
  3.7 8.9 %all-to-all-start = ((s32[32,3,2]{1,2,0:T(2,128)}), s32[32,3,2]{1,2,0:T(2,128)S(1)}, u32[]{:S(2)}, u32[]{:S(2)}) async-start(s32[32,3,2]{1,2,0:T(2,128)} %copy.70), calls=%async_computation | async-start | bytes 65536 | tf_op jit(solution)/shard_map/all_to_all | solution.py:261
  12.6 5.6 %all-to-all-done = s32[32,3,2]{1,2,0:T(2,128)S(1)} async-done(((s32[32,3,2]{1,2,0:T(2,128)}), s32[32,3,2]{1,2,0:T(2,128)S(1)}, u32[]{:S(2)}, u32[]{:S(2)}) %all-to-all-start) | async-done | bytes 800 | tf_op jit(solution)/shard_map/all_to_all | solution.py:261
  19.3 7.2 %pick_own.1 = bf16[8,2,2,2,32,1536]{5,4,3,2,1,0:T(8,128)(2,1)} custom-call(s32[8,2,2]{2,1,0:T(2,128)} %copy.72.ids, bf16[24,32,1536]{2,1,0:T(8,128)(2,1)} %bitcast.35, bf16[24,32,1536]{2,1,0:T(8,128)(2,1)} %bitcast.39), custom_call_target="tpu_custom_call" | custom-call | bytes 12582912 | tf_op jit(solution)/shard_map/pick_own/pallas_call | solution.py:203
  26.5 6.5 %all-to-all-start.1 = ((bf16[8,2,2,2,32,1536]{5,4,3,2,1,0:T(8,128)(2,1)}), bf16[8,2,2,2,32,1536]{5,4,3,2,1,0:T(8,128)(2,1)}, u32[]{:S(2)}, u32[]{:S(2)}) async-start(bf16[8,2,2,2,32,1536]{5,4,3,2,1,0:T(8,128)(2,1)} %pick_own.1), calls=%async_computation.1 | async-start | bytes 12582912 | tf_op jit(solution)/shard_map/all_to_all | solution.py:266
  33.3 2.3 collective-permute-start.1
  35.6 2.7 collective-permute-start.3
  38.3 2.2 collective-permute-start.5
  42.3 42.4 %collective-permute-done = bf16[2,384,1536]{2,1,0:T(8,128)(2,1)S(1)} collective-permute-done((bf16[2,384,1536]{2,1,0:T(8,128)(2,1)}, bf16[2,384,1536]{2,1,0:T(8,128)(2,1)S(1)}, u32[]{:S(2)}, u32[]{:S(2)}) %collective-permute-start) | collective-permute-done | bytes 2359328 | tf_op jit(solution)/shard_map/ppermute | solution.py:247
  84.7 10.8 %collective-permute-start.6 = (bf16[384,1536]{1,0:T(8,128)(2,1)S(1)}, bf16[384,1536]{1,0:T(8,128)(2,1)S(1)}, u32[]{:S(2)}, u32[]{:S(2)}) collective-permute-start(bf16[384,1536]{1,0:T(8,128)(2,1)S(1)} %get-tuple-element.40), channel_id=1, source_target_pairs={{0,32},{32,64},{64,96},{1,33},{33,65},{65,97},{2,34},{34,66},{66,9... | collective-permute-start | bytes 3538952 | tf_op jit(solution)/shard_map/ppermute | solution.py:246
  97.2 2.5 collective-permute-start.4
  99.7 20.0 %collective-permute-done.6.qu = bf16[384,1536]{1,0:T(8,128)(2,1)S(1)} collective-permute-done((bf16[384,1536]{1,0:T(8,128)(2,1)S(1)}, bf16[384,1536]{1,0:T(8,128)(2,1)S(1)}, u32[]{:S(2)}, u32[]{:S(2)}) %collective-permute-start.6) | collective-permute-done | bytes 1179680 | tf_op jit(solution)/shard_map/ppermute | solution.py:246
  122.5 17.4 %collective-permute-done.7.qd = bf16[384,1536]{1,0:T(8,128)(2,1)S(1)} collective-permute-done((bf16[384,1536]{1,0:T(8,128)(2,1)S(1)}, bf16[384,1536]{1,0:T(8,128)(2,1)S(1)}, u32[]{:S(2)}, u32[]{:S(2)}) %collective-permute-start.7) | collective-permute-done | bytes 1179680 | tf_op jit(solution)/shard_map/ppermute | solution.py:246
  139.9 46.0 %collective-permute-done.2 = bf16[2,384,1536]{2,1,0:T(8,128)(2,1)} collective-permute-done((bf16[2,384,1536]{2,1,0:T(8,128)(2,1)}, bf16[2,384,1536]{2,1,0:T(8,128)(2,1)}, u32[]{:S(2)}, u32[]{:S(2)}) %collective-permute-start.2) | collective-permute-done | bytes 2359328 | tf_op jit(solution)/shard_map/ppermute | solution.py:248
  185.9 7.1 %pick_near.1 = bf16[8,2,2,2,32,1536]{5,4,3,2,1,0:T(8,128)(2,1)} custom-call(s32[8,2,2]{2,1,0:T(2,128)} %copy.73.ids, bf16[24,32,1536]{2,1,0:T(8,128)(2,1)} %bitcast.32, bf16[24,32,1536]{2,1,0:T(8,128)(2,1)} %bitcast.14.refs_1_, bf16[24,32,1536]{2,1,0:T(8,128)(2,1)} %bitcast.15.refs_2_, bf16[24,32,1536]{2,1,0:T(8,128)(2,1)} %bitcast.16.refs_3_), custom_call_target="tpu_custom_call" | custom-call | bytes 12582912 | tf_op jit(solution)/shard_map/pick_near/pallas_call | solution.py:203
  193.0 5.3 %all-to-all-start.2 = ((bf16[8,2,2,2,32,1536]{5,4,3,2,1,0:T(8,128)(2,1)}), bf16[8,2,2,2,32,1536]{5,4,3,2,1,0:T(8,128)(2,1)}, u32[]{:S(2)}, u32[]{:S(2)}) async-start(bf16[8,2,2,2,32,1536]{5,4,3,2,1,0:T(8,128)(2,1)} %pick_near.1), calls=%async_computation.2 | async-start | bytes 12582912 | tf_op jit(solution)/shard_map/all_to_all | solution.py:272
  199.0 4.1 %slice_bitcast_fusion = bf16[8,2,2,32,1536]{4,3,2,1,0:T(8,128)(2,1)} fusion(bf16[8,2,2,2,32,1536]{5,4,3,2,1,0:T(8,128)(2,1)} %all-to-all-done.1.refs_0_.refs_1_), kind=kLoop, calls=%fused_computation | loop fusion | bytes 6291456 | tf_op jit(solution)/shard_map/squeeze | solution.py:267
  203.1 6.7 %broadcast_select_fusion = (bf16[2,384,1536]{2,1,0:T(8,128)(2,1)}, bf16[2,384,1536]{2,1,0:T(8,128)(2,1)}, bf16[2,384,1536]{2,1,0:T(8,128)(2,1)}, bf16[2,384,1536]{2,1,0:T(8,128)(2,1)}) fusion(bf16[2,384,1536]{2,1,0:T(8,128)(2,1)} %collective-permute-done.5, bf16[2,384,1536]{2,1,0:T(8,128)(2,1)} %collective-permute-done.3, pred[]{:T(512)S(6)} %eq.84, ...), kind=kLoop, calls=%fused_computation.1 | loop fusion | flops 4718592 | bytes 23592962 | tf_op jit(solution)/shard_map/jit(_where)/select_n | solution.py:274
  209.8 56.0 %window.1 = (f32[2,384,1536]{2,1,0:T(8,128)}, bf16[384,1536]{1,0:T(8,128)(2,1)}, bf16[384,1536]{1,0:T(8,128)(2,1)}, f32[2,384,128]{2,1,0:T(8,128)}, f32[384,128]{1,0:T(8,128)}, /*index=5*/f32[384,128]{1,0:T(8,128)}) custom-call(s32[2]{0:T(128)} %pad_add_fusion.5.place, bf16[2,384,1536]{2,1,0:T(8,128)(2,1)} %bitcast.33, bf16[384,1536]{1,0:T(8,128)(2,1)} %copy-done.6, ...), custom_call_target="tpu_custom_call" | custom-call | flops 16307453952 | bytes 31457280 | tf_op jit(solution)/shard_map/window/pallas_call | solution.py:82
  265.8 8.4 %collective-permute-start.10 = (bf16[384,1536]{1,0:T(8,128)(2,1)}, bf16[384,1536]{1,0:T(8,128)(2,1)}, u32[]{:S(2)}, u32[]{:S(2)}) collective-permute-start(bf16[384,1536]{1,0:T(8,128)(2,1)} %get-tuple-element.30), channel_id=1, source_target_pairs={{0,32},{32,64},{64,96},{1,33},{33,65},{65,97},{2,34},{34,66},{66,9... | collective-permute-start | bytes 3538952 | tf_op jit(solution)/shard_map/ppermute | solution.py:292
  274.2 1.9 collective-permute-start.9
  276.1 1.9 collective-permute-start.11
  278.1 5.1 %collective-permute-start.12 = (f32[384,128]{1,0:T(8,128)}, f32[384,128]{1,0:T(8,128)S(1)}, u32[]{:S(2)}, u32[]{:S(2)}) collective-permute-start(f32[384,128]{1,0:T(8,128)} %get-tuple-element.32), channel_id=1, source_target_pairs={{0,32},{32,64},{64,96},{1,33},{33,65},{65,97},{2,34},{34,66},{66,9... | collective-permute-start | bytes 589832 | tf_op jit(solution)/shard_map/ppermute | solution.py:292
  284.6 11.0 %collective-permute-done.11.refs_10_ = f32[384,128]{1,0:T(8,128)S(1)} collective-permute-done((f32[384,128]{1,0:T(8,128)}, f32[384,128]{1,0:T(8,128)S(1)}, u32[]{:S(2)}, u32[]{:S(2)}) %collective-permute-start.11) | collective-permute-done | bytes 196640 | tf_op jit(solution)/shard_map/ppermute | solution.py:291
  297.4 26.9 %cubes.1 = bf16[2,384,1536]{2,1,0:T(8,128)(2,1)} custom-call(s32[64]{0:T(128)} %select_reduce_fusion.1.slot_of, s32[2]{0:T(128)} %bitcast.47, s32[2]{0:T(128)} %add_convert_fusion.has, bf16[2,384,1536]{2,1,0:T(8,128)(2,1)} %bitcast.34, bf16[8,2,2,2,32,1536]{5,4,3,2,1,0:T(8,128)(2,1)} %all-to-all-done.1.refs_0_.refs_1_, ...), custom_call_target="tpu_custom_call" | custom-call | flops 4831838208 | bytes 20971520 | tf_op jit(solution)/shard_map/cubes/pallas_call | solution.py:154
  (65 shorter events, 15.2 us)
Async XLA Ops:
  3.7 14.5 %all-to-all-start = ((s32[32,3,2]{1,2,0:T(2,128)}), s32[32,3,2]{1,2,0:T(2,128)S(1)}, u32[]{:S(2)}, u32[]{:S(2)}) async-start(s32[32,3,2]{1,2,0:T(2,128)} %copy.70), calls=%async_computation | async-start | bytes 65536 | tf_op jit(solution)/shard_map/all_to_all | solution.py:261
  26.5 166.6 %all-to-all-start.1 = ((bf16[8,2,2,2,32,1536]{5,4,3,2,1,0:T(8,128)(2,1)}), bf16[8,2,2,2,32,1536]{5,4,3,2,1,0:T(8,128)(2,1)}, u32[]{:S(2)}, u32[]{:S(2)}) async-start(bf16[8,2,2,2,32,1536]{5,4,3,2,1,0:T(8,128)(2,1)} %pick_own.1), calls=%async_computation.1 | async-start | bytes 12582912 | tf_op jit(solution)/shard_map/all_to_all | solution.py:266
  32.9 51.8 %collective-permute-start = (bf16[2,384,1536]{2,1,0:T(8,128)(2,1)}, bf16[2,384,1536]{2,1,0:T(8,128)(2,1)S(1)}, u32[]{:S(2)}, u32[]{:S(2)}) collective-permute-start(bf16[2,384,1536]{2,1,0:T(8,128)(2,1)} %bitcast.36), channel_id=1, source_target_pairs={{0,1},{1,2},{2,3},{3,0},{4,5},{5,6},{6,7},{7,4},{8,9},{9,10},{10,1... | collective-permute-start | bytes 7077896 | tf_op jit(solution)/shard_map/ppermute | solution.py:247
  33.3 62.2 %collective-permute-start.1 = (bf16[2,384,1536]{2,1,0:T(8,128)(2,1)}, bf16[2,384,1536]{2,1,0:T(8,128)(2,1)}, u32[]{:S(2)}, u32[]{:S(2)}) collective-permute-start(bf16[2,384,1536]{2,1,0:T(8,128)(2,1)} %bitcast.37), channel_id=1, source_target_pairs={{1,0},{2,1},{3,2},{0,3},{5,4},{6,5},{7,6},{4,7},{9,8},{10,9},{11,1... | collective-permute-start | bytes 7077896 | tf_op jit(solution)/shard_map/ppermute | solution.py:247
  35.6 150.3 %collective-permute-start.2 = (bf16[2,384,1536]{2,1,0:T(8,128)(2,1)}, bf16[2,384,1536]{2,1,0:T(8,128)(2,1)}, u32[]{:S(2)}, u32[]{:S(2)}) collective-permute-start(bf16[2,384,1536]{2,1,0:T(8,128)(2,1)} %bitcast.40), channel_id=1, source_target_pairs={{0,1},{1,2},{2,3},{3,0},{4,5},{5,6},{6,7},{7,4},{8,9},{9,10},{10,1... | collective-permute-start | bytes 7077896 | tf_op jit(solution)/shard_map/ppermute | solution.py:248
  35.6 150.3 %collective-permute-start.3 = (bf16[2,384,1536]{2,1,0:T(8,128)(2,1)}, bf16[2,384,1536]{2,1,0:T(8,128)(2,1)}, u32[]{:S(2)}, u32[]{:S(2)}) collective-permute-start(bf16[2,384,1536]{2,1,0:T(8,128)(2,1)} %bitcast.41), channel_id=1, source_target_pairs={{1,0},{2,1},{3,2},{0,3},{5,4},{6,5},{7,6},{4,7},{9,8},{10,9},{11,1... | collective-permute-start | bytes 7077896 | tf_op jit(solution)/shard_map/ppermute | solution.py:248
  38.3 147.6 %collective-permute-start.5 = (bf16[2,384,1536]{2,1,0:T(8,128)(2,1)}, bf16[2,384,1536]{2,1,0:T(8,128)(2,1)}, u32[]{:S(2)}, u32[]{:S(2)}) collective-permute-start(bf16[2,384,1536]{2,1,0:T(8,128)(2,1)} %bitcast.42), channel_id=1, source_target_pairs={{3,4},{7,8},{11,12},{15,16},{19,20},{23,24},{27,28},{4,3},{8,7},{1... | collective-permute-start | bytes 7077896 | tf_op jit(solution)/shard_map/ppermute | solution.py:269
  84.7 12.5 %copy-start = (bf16[2,384,1536]{2,1,0:T(8,128)(2,1)}, bf16[2,384,1536]{2,1,0:T(8,128)(2,1)S(1)}, u32[]{:S(2)}) copy-start(bf16[2,384,1536]{2,1,0:T(8,128)(2,1)S(1)} %collective-permute-done) | copy-start | bytes 7077892
  84.7 35.0 %collective-permute-start.6 = (bf16[384,1536]{1,0:T(8,128)(2,1)S(1)}, bf16[384,1536]{1,0:T(8,128)(2,1)S(1)}, u32[]{:S(2)}, u32[]{:S(2)}) collective-permute-start(bf16[384,1536]{1,0:T(8,128)(2,1)S(1)} %get-tuple-element.40), channel_id=1, source_target_pairs={{0,32},{32,64},{64,96},{1,33},{33,65},{65,97},{2,34},{34,66},{66,9... | collective-permute-start | bytes 3538952 | tf_op jit(solution)/shard_map/ppermute | solution.py:246
  97.2 88.7 %collective-permute-start.4 = (bf16[2,384,1536]{2,1,0:T(8,128)(2,1)}, bf16[2,384,1536]{2,1,0:T(8,128)(2,1)}, u32[]{:S(2)}, u32[]{:S(2)}) collective-permute-start(bf16[2,384,1536]{2,1,0:T(8,128)(2,1)} %broadcast_select_fusion.4), channel_id=1, source_target_pairs={{0,4},{4,8},{8,12},{12,16},{16,20},{20,24},{24,28},{7,3},{11,7},{1... | collective-permute-start | bytes 7077896 | tf_op jit(solution)/shard_map/ppermute | solution.py:268
  119.7 1.9 copy-start.6
  119.7 20.2 %collective-permute-start.7 = (bf16[384,1536]{1,0:T(8,128)(2,1)S(1)}, bf16[384,1536]{1,0:T(8,128)(2,1)S(1)}, u32[]{:S(2)}, u32[]{:S(2)}) collective-permute-start(bf16[384,1536]{1,0:T(8,128)(2,1)S(1)} %get-tuple-element.39), channel_id=1, source_target_pairs={{32,0},{64,32},{96,64},{33,1},{65,33},{97,65},{34,2},{66,34},{98,6... | collective-permute-start | bytes 3538952 | tf_op jit(solution)/shard_map/ppermute | solution.py:246
  139.9 53.1 %copy-start.7 = (bf16[384,1536]{1,0:T(8,128)(2,1)}, bf16[384,1536]{1,0:T(8,128)(2,1)S(1)}, u32[]{:S(2)}) copy-start(bf16[384,1536]{1,0:T(8,128)(2,1)S(1)} %collective-permute-done.7.qd) | copy-start | bytes 3538948
  193.0 102.6 %all-to-all-start.2 = ((bf16[8,2,2,2,32,1536]{5,4,3,2,1,0:T(8,128)(2,1)}), bf16[8,2,2,2,32,1536]{5,4,3,2,1,0:T(8,128)(2,1)}, u32[]{:S(2)}, u32[]{:S(2)}) async-start(bf16[8,2,2,2,32,1536]{5,4,3,2,1,0:T(8,128)(2,1)} %pick_near.1), calls=%async_computation.2 | async-start | bytes 12582912 | tf_op jit(solution)/shard_map/all_to_all | solution.py:272
  199.0 4.1 %copy-start.1 = (bf16[2,384,1536]{2,1,0:T(8,128)(2,1)S(1)}, bf16[2,384,1536]{2,1,0:T(8,128)(2,1)}, u32[]{:S(2)}) copy-start(bf16[2,384,1536]{2,1,0:T(8,128)(2,1)} %copy-done) | copy-start | bytes 7077892
  203.1 92.5 %collective-permute-start.8 = (bf16[8,2,2,32,1536]{4,3,2,1,0:T(8,128)(2,1)}, bf16[8,2,2,32,1536]{4,3,2,1,0:T(8,128)(2,1)S(1)}, u32[]{:S(2)}, u32[]{:S(2)}) collective-permute-start(bf16[8,2,2,32,1536]{4,3,2,1,0:T(8,128)(2,1)} %slice_bitcast_fusion), channel_id=1, source_target_pairs={{0,2},{1,3},{2,0},{3,1},{4,6},{5,7},{6,4},{7,5},{8,10},{9,11},{10,... | collective-permute-start | bytes 9437192 | tf_op jit(solution)/shard_map/ppermute | solution.py:267
  209.8 74.1 %copy-start.5 = (s32[64]{0:T(128)S(1)}, s32[64]{0:T(128)}, u32[]{:S(2)}) copy-start(s32[64]{0:T(128)} %get-tuple-element.51) | copy-start | bytes 772
  265.8 29.8 %collective-permute-start.10 = (bf16[384,1536]{1,0:T(8,128)(2,1)}, bf16[384,1536]{1,0:T(8,128)(2,1)}, u32[]{:S(2)}, u32[]{:S(2)}) collective-permute-start(bf16[384,1536]{1,0:T(8,128)(2,1)} %get-tuple-element.30), channel_id=1, source_target_pairs={{0,32},{32,64},{64,96},{1,33},{33,65},{65,97},{2,34},{34,66},{66,9... | collective-permute-start | bytes 3538952 | tf_op jit(solution)/shard_map/ppermute | solution.py:292
  274.2 21.4 %collective-permute-start.9 = (bf16[384,1536]{1,0:T(8,128)(2,1)}, bf16[384,1536]{1,0:T(8,128)(2,1)}, u32[]{:S(2)}, u32[]{:S(2)}) collective-permute-start(bf16[384,1536]{1,0:T(8,128)(2,1)} %get-tuple-element.29), channel_id=1, source_target_pairs={{32,0},{64,32},{96,64},{33,1},{65,33},{97,65},{34,2},{66,34},{98,6... | collective-permute-start | bytes 3538952 | tf_op jit(solution)/shard_map/ppermute | solution.py:291
  276.1 19.4 %collective-permute-start.11 = (f32[384,128]{1,0:T(8,128)}, f32[384,128]{1,0:T(8,128)S(1)}, u32[]{:S(2)}, u32[]{:S(2)}) collective-permute-start(f32[384,128]{1,0:T(8,128)} %get-tuple-element.31), channel_id=1, source_target_pairs={{32,0},{64,32},{96,64},{33,1},{65,33},{97,65},{34,2},{66,34},{98,6... | collective-permute-start | bytes 589832 | tf_op jit(solution)/shard_map/ppermute | solution.py:291
  278.1 17.5 %collective-permute-start.12 = (f32[384,128]{1,0:T(8,128)}, f32[384,128]{1,0:T(8,128)S(1)}, u32[]{:S(2)}, u32[]{:S(2)}) collective-permute-start(f32[384,128]{1,0:T(8,128)} %get-tuple-element.32), channel_id=1, source_target_pairs={{0,32},{32,64},{64,96},{1,33},{33,65},{65,97},{2,34},{34,66},{66,9... | collective-permute-start | bytes 589832 | tf_op jit(solution)/shard_map/ppermute | solution.py:292
  295.5 0.7 copy-start.3
  295.5 0.7 copy-start.4
  295.6 1.8 copy-start.2

commit v3 on v2

v3 whole, which is shorter than its diff:
```python
import functools
import math

import jax
import jax.numpy as jnp
from jax import lax
from jax.experimental import pallas as pl
from jax.experimental.pallas import tpu as pltpu
from jax.sharding import PartitionSpec as P

HEAD = 128
CUBE = 32
LOG_SCALE = HEAD ** -0.5 * math.log2(math.e)
NEG = -1e30
VMEM = 56 << 20


def dot_t(a, b):
    return lax.dot_general(a, b, (((1,), (1,)), ((), ())), preferred_element_type=jnp.float32)


def dot(a, b):
    return lax.dot_general(a, b, (((1,), (0,)), ((), ())), preferred_element_type=jnp.float32)


def partial_softmax(scores, vals):
    top = functools.reduce(jnp.maximum, [jnp.max(s, axis=1, keepdims=True) for s in scores])
    total = 0.0
    mixed = 0.0
    for s, v in zip(scores, vals):
        w = jnp.exp2((s - top) * LOG_SCALE)
        total = total + jnp.sum(w, axis=1, keepdims=True)
        mixed = mixed + dot(w.astype(jnp.bfloat16), v)
    return mixed / total, top * LOG_SCALE + jnp.log2(total)


def window_kernel(rows_of, place, *refs):
    count = len(rows_of)
    queries, keys, vals = refs[:count], refs[count : count + 3], refs[count + 3 : count + 6]
    outs, levels = refs[count + 6 : 2 * count + 6], refs[2 * count + 6 :]
    head = pl.program_id(0)
    lane = lax.broadcasted_iota(jnp.int32, queries[0].shape, 1)

    def run(cols):
        for query, out, lse, rows in zip(queries, outs, levels, rows_of):
            picks = [(c, r) for c in cols for r in rows]
            scores = [dot_t(query[...], keys[c][r]) for c, r in picks]
            mixed, level = partial_softmax(scores, [vals[c][r] for c, r in picks])
            out[...] = mixed.astype(out.dtype)
            lse[...] = jnp.where(lane == head, level, lse[...])

    first = place[0] == 0
    last = place[0] == place[1] - 1

    @pl.when(jnp.logical_not(first | last))
    def _():
        run((0, 1, 2))

    @pl.when(first)
    def _():
        run((1, 2))

    @pl.when(last)
    def _():
        run((0, 1))


def window(place, queries, rows_of, keys, vals, dtype, name):
    tile, feat = queries[0].shape
    heads = feat // HEAD
    count = len(queries)
    tiles = 3 * sum(len(rows) for rows in rows_of)
    two = pl.BlockSpec((keys[0].shape[0], tile, HEAD), lambda h, *_: (0, 0, h))
    one = pl.BlockSpec((tile, HEAD), lambda h, *_: (0, h))
    level = pl.BlockSpec((tile, HEAD), lambda h, *_: (0, 0))
    shape = jax.ShapeDtypeStruct
    out = pl.pallas_call(
        functools.partial(window_kernel, rows_of),
        grid_spec=pltpu.PrefetchScalarGridSpec(
            num_scalar_prefetch=1,
            grid=(heads,),
            in_specs=[one] * count + [two] * 6,
            out_specs=[one] * count + [level] * count,
        ),
        out_shape=[shape((tile, feat), dtype)] * count + [shape((tile, HEAD), jnp.float32)] * count,
        compiler_params=pltpu.CompilerParams(vmem_limit_bytes=VMEM),
        cost_estimate=pl.CostEstimate(
            flops=4 * tile * tiles * tile * feat, bytes_accessed=20 << 20, transcendentals=tile * tiles * tile * heads
        ),
        name=name,
    )(place, *queries, *keys, *vals)
    return out[:count], out[count:]


def cube_kernel(slot_of, counts, has, q, *refs):
    sources, (o0, o1, lo0, lo1, ou, od, lu, ld, out, kbuf, vbuf) = refs[:6], refs[6:]
    rows, tile, width = q.shape
    lane = lax.broadcasted_iota(jnp.int32, (tile, HEAD), 1)
    index = 0
    for ck, cv in (sources[0:2], sources[2:4], sources[4:6]):
        for at in range(ck.shape[0]):
            for rank in range(ck.shape[1]):
                spot = pl.ds(pl.multiple_of(slot_of[index] * CUBE, CUBE), CUBE)
                kbuf[spot, :] = ck[at, rank]
                vbuf[spot, :] = cv[at, rank]
                index += 1
    span = index * CUBE // rows
    half = span // 2
    slot = half // CUBE + lax.broadcasted_iota(jnp.int32, (1, half), 1) // CUBE
    for part in range(width // HEAD):
        lanes = slice(part * HEAD, (part + 1) * HEAD)
        head = pl.program_id(0) * (width // HEAD) + part

        def column(x):
            return jnp.sum(jnp.where(lane == head, x, 0.0), axis=1, keepdims=True)

        scores = []
        for t in range(rows):
            live = dot_t(q[t, :, lanes], kbuf[pl.ds(t * span, half), lanes])
            rest = dot_t(q[t, :, lanes], kbuf[pl.ds(t * span + half, half), lanes])
            scores.append((live, jnp.where(slot < counts[t], rest, NEG)))
        for t, (o, lo, ext, lext) in enumerate(((o0, lo0, od, ld), (o1, lo1, ou, lu))):
            vals = [vbuf[pl.ds(t * span + i * half, half), lanes] for i in range(2)]
            mixed, level = partial_softmax(scores[t], vals)
            win_level = column(lo[...])
            ext_level = jnp.where(has[t] > 0, column(lext[...]), NEG)
            top = jnp.maximum(jnp.maximum(level, win_level), ext_level)
            a = jnp.exp2(level - top)
            b = jnp.exp2(win_level - top)
            c = jnp.exp2(ext_level - top)
            norm = 1.0 / (a + b + c)
            mixed = mixed * (a * norm) + o[:, lanes] * (b * norm) + ext[:, lanes].astype(jnp.float32) * (c * norm)
            out[t, :, lanes] = mixed.astype(out.dtype)


def cubes(slot_of, counts, has, q, early, near, far, o, lo, ou, od, lu, ld):
    rows, tile, feat = q.shape
    heads = feat // HEAD
    width = 2 * HEAD
    keys = slot_of.shape[0] * CUBE
    two = pl.BlockSpec((rows, tile, width), lambda h, *_: (0, 0, h))
    one = pl.BlockSpec((tile, width), lambda h, *_: (0, h))
    one_c = pl.BlockSpec((tile, HEAD), lambda h, *_: (0, 0))

    def block(x, kv):
        return pl.BlockSpec((x.shape[0], None, 1, CUBE, width), lambda h, *_: (0, kv, 0, 0, h))

    mine = pl.BlockSpec((early.shape[0], None, None, 1, CUBE, width), lambda h, *_: (0, 2, 0, 0, 0, h))
    mine_v = pl.BlockSpec((early.shape[0], None, None, 1, CUBE, width), lambda h, *_: (0, 2, 1, 0, 0, h))
    near, far = (x.reshape((-1,) + x.shape[2:]) for x in (near, far))
    return pl.pallas_call(
        cube_kernel,
        grid_spec=pltpu.PrefetchScalarGridSpec(
            num_scalar_prefetch=3,
            grid=(feat // width,),
            in_specs=[two]
            + [mine, mine_v]
            + [block(x, kv) for x in (near, far) for kv in range(2)]
            + [one, one, one_c, one_c, one, one, one_c, one_c],
            out_specs=two,
            scratch_shapes=[pltpu.VMEM((keys, width), jnp.bfloat16)] * 2,
        ),
        out_shape=jax.ShapeDtypeStruct((rows, tile, feat), jnp.bfloat16),
        compiler_params=pltpu.CompilerParams(vmem_limit_bytes=VMEM),
        cost_estimate=pl.CostEstimate(
            flops=4 * tile * keys * feat, bytes_accessed=20 << 20, transcendentals=tile * keys * heads
        ),
        name="cubes",
    )(slot_of, counts, has, q, early, early, near, near, far, far, *o, *lo, ou, od, lu, ld)


def pick_kernel(ids, *refs):
    tables, (out, held, into, back) = refs[:-4], refs[-4:]
    groups, sides, kinds, ranks = out.shape[:4]
    pairs = []
    for g in range(groups):
        for s in range(sides):
            for kv in range(kinds):
                table = tables[kv if len(tables) == kinds else s * kinds + kv]
                for r in range(ranks):
                    at = len(pairs)
                    pairs.append(
                        (
                            pltpu.make_async_copy(table.at[ids[g, s, r]], held.at[at], into.at[at]),
                            pltpu.make_async_copy(held.at[at], out.at[g, s, kv, r], back.at[at]),
                        )
                    )
    for read, _ in pairs:
        read.start()
    for read, write in pairs:
        read.wait()
        write.start()
    for _, write in pairs:
        write.wait()


def pick(ids, tables, kinds, name):
    feat = tables[0].shape[-1]
    shape = ids.shape[:2] + (kinds,) + ids.shape[2:] + (CUBE, feat)
    tables = [x.reshape(-1, CUBE, feat) for x in tables]
    return pl.pallas_call(
        pick_kernel,
        grid_spec=pltpu.PrefetchScalarGridSpec(
            num_scalar_prefetch=1,
            grid=(1,),
            in_specs=[pl.BlockSpec(memory_space=pl.ANY)] * len(tables),
            out_specs=pl.BlockSpec(memory_space=pl.ANY),
            scratch_shapes=[
                pltpu.VMEM((math.prod(shape[:4]), CUBE, feat), tables[0].dtype),
                pltpu.SemaphoreType.DMA((math.prod(shape[:4]),)),
                pltpu.SemaphoreType.DMA((math.prod(shape[:4]),)),
            ],
        ),
        out_shape=jax.ShapeDtypeStruct(shape, tables[0].dtype),
        compiler_params=pltpu.CompilerParams(vmem_limit_bytes=VMEM),
        cost_estimate=pl.CostEstimate(flops=0, bytes_accessed=4 * math.prod(shape), transcendentals=0),
        name=name,
    )(ids, *tables)


DEPTH = 4


def body(queries, keys, values, selected, counts):
    rows = queries.shape[0]
    tile = queries.shape[2]
    feat = queries.shape[3]
    slots = selected.shape[2]
    columns = lax.axis_size("wa")
    bands = lax.axis_size("ha")
    cubes_dev = rows * (tile // CUBE)
    q, k, v = (x[:, 0] for x in (queries, keys, values))
    down = [(i, i + 1) for i in range(bands - 1)]
    up = [(i + 1, i) for i in range(bands - 1)]
    lines = columns // DEPTH
    planes = [[line * DEPTH + z for line in range(lines)] for z in range(DEPTH)]
    right = [(i, (i + 1) % columns) for i in range(columns)]
    left = [(j, i) for i, j in right]
    spin = [(i, i - i % DEPTH + (i + 1) % DEPTH) for i in range(columns)]
    spun = [(j, i) for i, j in spin]
    across = [(i, i - i % DEPTH + (i + 2) % DEPTH) for i in range(columns)]
    onto = [(i, (i + DEPTH) % columns) for i in range(0, columns, DEPTH)]
    onto = onto + [(j + DEPTH - 1, i + DEPTH - 1) for i, j in onto]
    col = lax.axis_index("wa")
    z = col % DEPTH

    ids = selected.reshape(rows * slots)
    owner = ids // cubes_dev
    local = ids % cubes_dev
    same = owner[:, None] == owner[None, :]
    before = jnp.arange(rows * slots)[:, None] > jnp.arange(rows * slots)[None, :]
    rank = jnp.sum((same & before).astype(jnp.int32), axis=1)
    place_at = (owner * 2 + rank)[:, None] == jnp.arange(columns * 2, dtype=jnp.int32)[None, :]
    wanted = jnp.sum(jnp.where(place_at, local[:, None], 0), axis=0).reshape(columns, 2)
    wanted = jnp.stack([jnp.roll(wanted, 1, axis=0), wanted, jnp.roll(wanted, -1, axis=0)], axis=1)
    asked = lax.all_to_all(wanted, "wa", split_axis=0, concat_axis=0, tiled=True)
    q_next, v_next, asked = lax.optimization_barrier((q, v, asked))
    qu, qd = lax.ppermute(q_next[1], "ha", down), lax.ppermute(q_next[0], "ha", up)
    vl, vr = lax.ppermute(v_next, "wa", spin), lax.ppermute(v_next, "wa", spun)
    asked = asked.reshape(lines, DEPTH, 3, 2)
    asked_same = lax.dynamic_index_in_dim(asked, z, 1, keepdims=False)
    asked_far = lax.dynamic_index_in_dim(asked, (z + 2) % DEPTH, 1, keepdims=False)
    early = jnp.stack([asked_far[:, 1, 0], asked_far[:, 1, 1], asked_same[:, 1, 0]], axis=1)
    early = pick(early[:, :, None], [k, v] * 3, 2, "pick_early")
    early = lax.all_to_all(early, "wa", split_axis=0, concat_axis=0, tiled=True, axis_index_groups=planes)
    wrap, early = lax.optimization_barrier((jnp.where(z == 0, vl, vr), early))
    vb = lax.ppermute(wrap, "wa", onto)
    k_next, _, _ = lax.optimization_barrier((k, vl, vr))
    kl, kr = lax.ppermute(k_next, "wa", right), lax.ppermute(k_next, "wa", left)
    vl, vr = jnp.where(z == 0, vb, vl), jnp.where(z == DEPTH - 1, vb, vr)
    far = lax.ppermute(early[:, :2], "wa", across)
    kl, kr, vl, vr, qu, qd = lax.optimization_barrier((kl, kr, vl, vr, qu, qd))
    late = jnp.concatenate([asked_same[:, 0], asked_same[:, 1, 1:], asked_same[:, 2]], axis=1)
    near = pick(late[:, :, None], [kl, vl, kl, vl, k, v, kr, vr, kr, vr], 2, "pick_near")
    near = lax.all_to_all(near, "wa", split_axis=0, concat_axis=0, tiled=True, axis_index_groups=planes)

    ahead = (owner - z) % DEPTH
    line = ((owner - jnp.where(ahead == 1, 1, 0) + jnp.where(ahead == 3, 1, 0)) % columns) // DEPTH
    near_at = jnp.where(ahead == 0, 2, jnp.where(ahead == 1, 3 + rank, rank))
    spot = jnp.where(
        ahead == 2, 6 * lines + line * 2 + rank, jnp.where((ahead == 0) & (rank == 0), line, lines + line * 5 + near_at)
    )
    entry = jnp.arange(rows * slots, dtype=jnp.int32)
    slot_of = jnp.sum(jnp.where(spot[:, None] == entry[None, :], entry[:, None], 0), axis=0)

    row = lax.axis_index("ha")
    place = jnp.stack([col, jnp.int32(columns)]).astype(jnp.int32)
    has = jnp.stack([row > 0, row < bands - 1]).astype(jnp.int32)
    near_keys, near_vals = (kl, k, kr), (vl, v, vr)
    edge, edge_level = window(place, (qu, qd), ((0,), (1,)), near_keys, near_vals, jnp.bfloat16, "window_edge")
    ou, lu = lax.ppermute(edge[0], "ha", up), lax.ppermute(edge_level[0], "ha", up)
    od, ld = lax.ppermute(edge[1], "ha", down), lax.ppermute(edge_level[1], "ha", down)
    o, lo = window(place, (q[0], q[1]), ((0, 1), (0, 1)), near_keys, near_vals, jnp.float32, "window_own")
    out = cubes(slot_of, counts[:, 0], has, q, early, near, far, o, lo, ou, od, lu, ld)
    return out[:, None]


def solution(mesh):
    return jax.shard_map(
        body,
        mesh=mesh,
        in_specs=(
            P("ha", "wa", None, None),
            P("ha", "wa", None, None),
            P("ha", "wa", None, None),
            P("ha", "wa", None),
            P("ha", "wa"),
        ),
        out_specs=P("ha", "wa", None, None),
        check_vma=False,
    )
```

time: 328 us -> 301 us (0.918)
  waiting for transfers between devices: 142 us -> 115 us
  starting transfers between devices: 60.8 us -> 52.6 us
  local copies, waits for them, and re-layouts: 11 us -> 17.1 us
    ppermute x13 -> x12, waiting for transfers between devices: 137 us -> 100 us  [the longest x1 49.2 us: body(): lax.ppermute(v_next, 'wa', spin)]
    all_to_all x1, waiting for transfers between devices: 0.01 us -> 8.95 us  [body(): lax.all_to_all(early, 'wa', split_axis=0, concat_axis=0, tiled=True, axis...]
    ppermute x13 -> x12, starting transfers between devices: 40.1 us -> 32.6 us  [the longest x1 8.1 us: body(): lax.ppermute(q_next[1], 'ha', down)]
    pallas_call x1 -> x2, Pallas kernels: 56 us -> 62 us  [window(): pl.pallas_call(functools.partial(window_kernel, rows_of), grid_spec=pltpu...]
    slice x3 -> x11, local copies, waits for them, and re-layouts: 0.09 us -> 5.54 us  [the longest x1 4.08 us: body(): far = lax.ppermute(early[:, :2], 'wa', across)]
    pallas_call x1, Pallas kernels: 26.9 us -> 21.5 us  [cubes(): pl.pallas_call(cube_kernel, grid_spec=pltpu.PrefetchScalarGridSpec(num_sc...]
  transfers between devices with their start and end apart: 16 -> 15, of which waited for: 6 -> 8; matrix products, arithmetic and copies ran while one was open for 5% -> 8% of each run, Pallas kernels for 19% -> 21%
where the time goes in v3:
time: 301 us; the launch traced here: 296 us
  waiting for transfers between devices  115 us (38%)
  Pallas kernels  98.4 us (33%)
  starting transfers between devices  52.6 us (17%)
  local copies, waits for them, and re-layouts  17.1 us (6%)
  other arithmetic  13.1 us (4%)
    pallas_call x2, Pallas kernels, window(): pl.pallas_call(functools.partial(window_kernel, rows_of), grid_spec=pltpu...  62 us
    ppermute x1, waiting for transfers between devices, body(): lax.ppermute(v_next, 'wa', spin)  49.2 us
    ppermute x1, waiting for transfers between devices, body(): vb = lax.ppermute(wrap, 'wa', onto)  29.2 us
    pallas_call x1, Pallas kernels, cubes(): pl.pallas_call(cube_kernel, grid_spec=pltpu.PrefetchScalarGridSpec(num_sc...  21.5 us
    pallas_call x2, Pallas kernels, pick(): pl.pallas_call(pick_kernel, grid_spec=pltpu.PrefetchScalarGridSpec(num_sc...  14.8 us
    ppermute x1, waiting for transfers between devices, body(): lax.ppermute(q_next[1], 'ha', down)  14 us
    all_to_all x1, waiting for transfers between devices, body(): lax.all_to_all(early, 'wa', split_axis=0, concat_axis=0, tiled=True, axis...  8.95 us
    all_to_all x1, starting transfers between devices, body(): lax.all_to_all(wanted, 'wa', split_axis=0, concat_axis=0, tiled=True)  8.86 us
  transfers between devices with their start and end apart: 15, of which 8 were waited for; matrix products, arithmetic and copies ran while one was open for 8% of the time, Pallas kernels for 21%

profile of v3, /device:TPU:7, one launch (start us, length us, event | category | flops | bytes accessed | tf_op | source)
XLA Modules:
  0.0 296.5 jit_solution(11768043842915434265)
XLA Ops:
  4.2 8.9 %all-to-all-start = ((s32[32,3,2]{1,2,0:T(2,128)}), s32[32,3,2]{1,2,0:T(2,128)S(1)}, u32[]{:S(2)}, u32[]{:S(2)}) async-start(s32[32,3,2]{1,2,0:T(2,128)} %copy.56), calls=%async_computation | async-start | bytes 65536 | tf_op jit(solution)/shard_map/all_to_all | solution.py:256
  13.1 5.6 %all-to-all-done = s32[32,3,2]{1,2,0:T(2,128)S(1)} async-done(((s32[32,3,2]{1,2,0:T(2,128)}), s32[32,3,2]{1,2,0:T(2,128)S(1)}, u32[]{:S(2)}, u32[]{:S(2)}) %all-to-all-start) | async-done | bytes 800 | tf_op jit(solution)/shard_map/all_to_all | solution.py:256
  20.4 6.0 %pick_early.1 = bf16[8,3,2,1,32,1536]{5,4,3,2,1,0:T(8,128)(2,1)} custom-call(s32[8,3,1]{2,1,0:T(4,128)} %copy.58.ids, bf16[24,32,1536]{2,1,0:T(8,128)(2,1)} %bitcast.49, bf16[24,32,1536]{2,1,0:T(8,128)(2,1)} %bitcast.15.refs_1_.refs_3_.refs_5_, bf16[24,32,1536]{2,1,0:T(8,128)(2,1)} %bitcast.50, bf16[24,32,1536]{2,1,0:T(8,128)(2,1)} %bitcast.15.refs_1_.refs_3_.refs_5_, ...), custom_call_target="tpu_custom_call" | custom-call | bytes 9437184 | tf_op jit(solution)/shard_map/pick_early/pallas_call | solution.py:201
  26.5 6.4 %all-to-all-start.1 = ((bf16[8,3,2,1,32,1536]{5,4,3,2,1,0:T(8,128)(2,1)}), bf16[8,3,2,1,32,1536]{5,4,3,2,1,0:T(8,128)(2,1)}, u32[]{:S(2)}, u32[]{:S(2)}) async-start(bf16[8,3,2,1,32,1536]{5,4,3,2,1,0:T(8,128)(2,1)} %pick_early.1), calls=%async_computation.1 | async-start | bytes 9437184 | tf_op jit(solution)/shard_map/all_to_all | solution.py:265
  33.1 2.4 collective-permute-start.1
  35.5 49.2 %collective-permute-done = bf16[2,384,1536]{2,1,0:T(8,128)(2,1)} collective-permute-done((bf16[2,384,1536]{2,1,0:T(8,128)(2,1)}, bf16[2,384,1536]{2,1,0:T(8,128)(2,1)}, u32[]{:S(2)}, u32[]{:S(2)}) %collective-permute-start) | collective-permute-done | bytes 2359328 | tf_op jit(solution)/shard_map/ppermute | solution.py:259
  84.7 3.3 %broadcast_select_fusion.2 = bf16[2,384,1536]{2,1,0:T(8,128)(2,1)} fusion(bf16[2,384,1536]{2,1,0:T(8,128)(2,1)} %collective-permute-done, bf16[2,384,1536]{2,1,0:T(8,128)(2,1)} %collective-permute-done.1, pred[]{:T(512)S(6)} %eq.96), kind=kLoop, calls=%fused_computation.2 | loop fusion | flops 1179648 | bytes 7077889 | tf_op jit(solution)/shard_map/jit(_where)/select_n | solution.py:266
  88.1 8.9 %all-to-all-done.1.refs_0_.refs_1_ = bf16[8,3,2,1,32,1536]{5,4,3,2,1,0:T(8,128)(2,1)} async-done(((bf16[8,3,2,1,32,1536]{5,4,3,2,1,0:T(8,128)(2,1)}), bf16[8,3,2,1,32,1536]{5,4,3,2,1,0:T(8,128)(2,1)}, u32[]{:S(2)}, u32[]{:S(2)}) %all-to-all-start.1) | async-done | bytes 4718624 | tf_op jit(solution)/shard_map/all_to_all | solution.py:265
  99.7 2.9 collective-permute-start.3
  102.6 2.9 slice_bitcast_fusion.2
  105.4 8.1 %collective-permute-start.5 = (bf16[384,1536]{1,0:T(8,128)(2,1)}, bf16[384,1536]{1,0:T(8,128)(2,1)}, u32[]{:S(2)}, u32[]{:S(2)}) collective-permute-start(bf16[384,1536]{1,0:T(8,128)(2,1)} %get-tuple-element.50), channel_id=1, source_target_pairs={{0,32},{32,64},{64,96},{1,33},{33,65},{65,97},{2,34},{34,66},{66,9... | collective-permute-start | bytes 3538952 | tf_op jit(solution)/shard_map/ppermute | solution.py:258
  119.7 29.2 %collective-permute-done.4 = bf16[2,384,1536]{2,1,0:T(8,128)(2,1)} collective-permute-done((bf16[2,384,1536]{2,1,0:T(8,128)(2,1)}, bf16[2,384,1536]{2,1,0:T(8,128)(2,1)}, u32[]{:S(2)}, u32[]{:S(2)}) %collective-permute-start.4) | collective-permute-done | bytes 2359328 | tf_op jit(solution)/shard_map/ppermute | solution.py:267
  148.9 4.9 %broadcast_select_fusion = (bf16[2,384,1536]{2,1,0:T(8,128)(2,1)}, bf16[2,384,1536]{2,1,0:T(8,128)(2,1)}) fusion(bf16[2,384,1536]{2,1,0:T(8,128)(2,1)} %collective-permute-done.4, bf16[2,384,1536]{2,1,0:T(8,128)(2,1)} %collective-permute-done.1, pred[]{:T(512)S(6)} %eq.99, bf16[2,384,1536]{2,1,0:T(8,128)(2,1)} %collective-permute-done, pred[]{:T(512)S(6)} %eq.96), kind=kLoop, calls=%fused_computation | loop fusion | flops 2359296 | bytes 11796482 | tf_op jit(solution)/shard_map/jit(_where)/select_n | solution.py:270
  153.8 14.0 %collective-permute-done.5.refs_0_ = bf16[384,1536]{1,0:T(8,128)(2,1)} collective-permute-done((bf16[384,1536]{1,0:T(8,128)(2,1)}, bf16[384,1536]{1,0:T(8,128)(2,1)}, u32[]{:S(2)}, u32[]{:S(2)}) %collective-permute-start.5) | collective-permute-done | bytes 1179680 | tf_op jit(solution)/shard_map/ppermute | solution.py:258
  167.8 3.1 %collective-permute-done.6.refs_1_ = bf16[384,1536]{1,0:T(8,128)(2,1)} collective-permute-done((bf16[384,1536]{1,0:T(8,128)(2,1)S(1)}, bf16[384,1536]{1,0:T(8,128)(2,1)}, u32[]{:S(2)}, u32[]{:S(2)}) %collective-permute-start.6) | collective-permute-done | bytes 1179680 | tf_op jit(solution)/shard_map/ppermute | solution.py:258
  170.9 8.8 %pick_near.1 = bf16[8,5,2,1,32,1536]{5,4,3,2,1,0:T(8,128)(2,1)} custom-call(s32[8,5,1]{2,1,0:T(8,128)} %copy.60.ids, bf16[24,32,1536]{2,1,0:T(8,128)(2,1)} %bitcast.23.refs_0_.refs_2_, bf16[24,32,1536]{2,1,0:T(8,128)(2,1)} %bitcast.59, bf16[24,32,1536]{2,1,0:T(8,128)(2,1)} %bitcast.23.refs_0_.refs_2_, bf16[24,32,1536]{2,1,0:T(8,128)(2,1)} %bitcast.60, ...), custom_call_target="tpu_custom_call" | custom-call | bytes 15728640 | tf_op jit(solution)/shard_map/pick_near/pallas_call | solution.py:201
  179.6 4.9 %all-to-all-start.2 = ((bf16[8,5,2,1,32,1536]{5,4,3,2,1,0:T(8,128)(2,1)}), bf16[8,5,2,1,32,1536]{5,4,3,2,1,0:T(8,128)(2,1)}, u32[]{:S(2)}, u32[]{:S(2)}) async-start(bf16[8,5,2,1,32,1536]{5,4,3,2,1,0:T(8,128)(2,1)} %pick_near.1), calls=%async_computation.2 | async-start | bytes 15728640 | tf_op jit(solution)/shard_map/all_to_all | solution.py:275
  184.5 4.1 %slice.95 = bf16[8,2,2,1,32,1536]{5,4,3,2,1,0:T(8,128)(2,1)} slice(bf16[8,3,2,1,32,1536]{5,4,3,2,1,0:T(8,128)(2,1)} %all-to-all-done.1.refs_0_.refs_1_), slice={[0:8], [0:2], [0:2], [0:1], [0:32], [0:1536]} | slice | bytes 6291456 | tf_op jit(solution)/shard_map/slice | solution.py:271
  190.8 23.3 %window_edge.1 = (bf16[384,1536]{1,0:T(8,128)(2,1)}, bf16[384,1536]{1,0:T(8,128)(2,1)}, f32[384,128]{1,0:T(8,128)}, f32[384,128]{1,0:T(8,128)}) custom-call(s32[2]{0:T(128)} %pad_add_fusion.1.place, bf16[384,1536]{1,0:T(8,128)(2,1)} %collective-permute-done.5.refs_0_, bf16[384,1536]{1,0:T(8,128)(2,1)} %collective-permute-done.6.refs_1_, ...), custom_call_target="tpu_custom_call" | custom-call | flops 5435817984 | bytes 20971520 | tf_op jit(solution)/shard_map/window_edge/pallas_call | solution.py:77
  216.0 5.1 %collective-permute-start.9 = (bf16[384,1536]{1,0:T(8,128)(2,1)}, bf16[384,1536]{1,0:T(8,128)(2,1)S(1)}, u32[]{:S(2)}, u32[]{:S(2)}) collective-permute-start(bf16[384,1536]{1,0:T(8,128)(2,1)} %get-tuple-element.42), channel_id=1, source_target_pairs={{0,32},{32,64},{64,96},{1,33},{33,65},{65,97},{2,34},{34,66},{66,9... | collective-permute-start | bytes 3538952 | tf_op jit(solution)/shard_map/ppermute | solution.py:292
  224.3 5.3 %collective-permute-start.11 = (f32[384,128]{1,0:T(8,128)}, f32[384,128]{1,0:T(8,128)S(1)}, u32[]{:S(2)}, u32[]{:S(2)}) collective-permute-start(f32[384,128]{1,0:T(8,128)} %get-tuple-element.44), channel_id=1, source_target_pairs={{0,32},{32,64},{64,96},{1,33},{33,65},{65,97},{2,34},{34,66},{66,9... | collective-permute-start | bytes 589832 | tf_op jit(solution)/shard_map/ppermute | solution.py:292
  229.6 38.8 %window_own.1 = (f32[384,1536]{1,0:T(8,128)}, f32[384,1536]{1,0:T(8,128)}, f32[384,128]{1,0:T(8,128)}, f32[384,128]{1,0:T(8,128)}) custom-call(s32[2]{0:T(128)} %pad_add_fusion.1.place, bf16[384,1536]{1,0:T(8,128)(2,1)} %get-tuple-element.48.refs_0_, bf16[384,1536]{1,0:T(8,128)(2,1)} %get-tuple-element.47.refs_1_, ...), custom_call_target="tpu_custom_call" | custom-call | flops 10871635968 | bytes 20971520 | tf_op jit(solution)/shard_map/window_own/pallas_call | solution.py:77
  268.4 4.1 %collective-permute-done.10.refs_12_ = f32[384,128]{1,0:T(8,128)S(1)} collective-permute-done((f32[384,128]{1,0:T(8,128)}, f32[384,128]{1,0:T(8,128)S(1)}, u32[]{:S(2)}, u32[]{:S(2)}) %collective-permute-start.10) | collective-permute-done | bytes 196640 | tf_op jit(solution)/shard_map/ppermute | solution.py:291
  274.8 21.5 %cubes.1 = bf16[2,384,1536]{2,1,0:T(8,128)(2,1)} custom-call(s32[64]{0:T(128)} %select_reduce_fusion.1.slot_of, s32[2]{0:T(128)} %bitcast.70, s32[2]{0:T(128)} %add_convert_fusion.has, bf16[2,384,1536]{2,1,0:T(8,128)(2,1)} %bitcast.62, bf16[8,3,2,1,32,1536]{5,4,3,2,1,0:T(8,128)(2,1)} %all-to-all-done.1.refs_0_.refs_1_, ...), custom_call_target="tpu_custom_call" | custom-call | flops 4831838208 | bytes 20971520 | tf_op jit(solution)/shard_map/cubes/pallas_call | solution.py:151
  (69 shorter events, 24.4 us)
Async XLA Ops:
  4.2 14.5 %all-to-all-start = ((s32[32,3,2]{1,2,0:T(2,128)}), s32[32,3,2]{1,2,0:T(2,128)S(1)}, u32[]{:S(2)}, u32[]{:S(2)}) async-start(s32[32,3,2]{1,2,0:T(2,128)} %copy.56), calls=%async_computation | async-start | bytes 65536 | tf_op jit(solution)/shard_map/all_to_all | solution.py:256
  26.5 70.5 %all-to-all-start.1 = ((bf16[8,3,2,1,32,1536]{5,4,3,2,1,0:T(8,128)(2,1)}), bf16[8,3,2,1,32,1536]{5,4,3,2,1,0:T(8,128)(2,1)}, u32[]{:S(2)}, u32[]{:S(2)}) async-start(bf16[8,3,2,1,32,1536]{5,4,3,2,1,0:T(8,128)(2,1)} %pick_early.1), calls=%async_computation.1 | async-start | bytes 9437184 | tf_op jit(solution)/shard_map/all_to_all | solution.py:265
  32.8 51.9 %collective-permute-start = (bf16[2,384,1536]{2,1,0:T(8,128)(2,1)}, bf16[2,384,1536]{2,1,0:T(8,128)(2,1)}, u32[]{:S(2)}, u32[]{:S(2)}) collective-permute-start(bf16[2,384,1536]{2,1,0:T(8,128)(2,1)} %bitcast.4.refs_6_), channel_id=1, source_target_pairs={{0,1},{1,2},{2,3},{3,0},{4,5},{5,6},{6,7},{7,4},{8,9},{9,10},{10,1... | collective-permute-start | bytes 7077896 | tf_op jit(solution)/shard_map/ppermute | solution.py:259
  33.1 51.6 %collective-permute-start.1 = (bf16[2,384,1536]{2,1,0:T(8,128)(2,1)}, bf16[2,384,1536]{2,1,0:T(8,128)(2,1)}, u32[]{:S(2)}, u32[]{:S(2)}) collective-permute-start(bf16[2,384,1536]{2,1,0:T(8,128)(2,1)} %bitcast.4.refs_6_), channel_id=1, source_target_pairs={{1,0},{2,1},{3,2},{0,3},{5,4},{6,5},{7,6},{4,7},{9,8},{10,9},{11,1... | collective-permute-start | bytes 7077896 | tf_op jit(solution)/shard_map/ppermute | solution.py:259
  35.5 63.4 %copy-start = (bf16[2,1,384,1536]{3,2,1,0:T(8,128)(2,1)S(1)}, bf16[2,1,384,1536]{3,2,1,0:T(8,128)(2,1)}, u32[]{:S(2)}) copy-start(bf16[2,1,384,1536]{3,2,1,0:T(8,128)(2,1)} %param.6) | copy-start | bytes 7077892
  97.0 51.9 %collective-permute-start.4 = (bf16[2,384,1536]{2,1,0:T(8,128)(2,1)}, bf16[2,384,1536]{2,1,0:T(8,128)(2,1)}, u32[]{:S(2)}, u32[]{:S(2)}) collective-permute-start(bf16[2,384,1536]{2,1,0:T(8,128)(2,1)} %broadcast_select_fusion.2), channel_id=1, source_target_pairs={{0,4},{4,8},{8,12},{12,16},{16,20},{20,24},{24,28},{28,0},{7,3},{1... | collective-permute-start | bytes 7077896 | tf_op jit(solution)/shard_map/ppermute | solution.py:267
  98.9 71.9 %collective-permute-start.2 = (bf16[2,384,1536]{2,1,0:T(8,128)(2,1)S(1)}, bf16[2,384,1536]{2,1,0:T(8,128)(2,1)}, u32[]{:S(2)}, u32[]{:S(2)}) collective-permute-start(bf16[2,384,1536]{2,1,0:T(8,128)(2,1)S(1)} %bitcast.55), channel_id=1, source_target_pairs={{0,1},{1,2},{2,3},{3,4},{4,5},{5,6},{6,7},{7,8},{8,9},{9,10},{10,1... | collective-permute-start | bytes 7077896 | tf_op jit(solution)/shard_map/ppermute | solution.py:269
  99.7 71.2 %collective-permute-start.3 = (bf16[2,384,1536]{2,1,0:T(8,128)(2,1)S(1)}, bf16[2,384,1536]{2,1,0:T(8,128)(2,1)}, u32[]{:S(2)}, u32[]{:S(2)}) collective-permute-start(bf16[2,384,1536]{2,1,0:T(8,128)(2,1)S(1)} %bitcast.56), channel_id=1, source_target_pairs={{1,0},{2,1},{3,2},{4,3},{5,4},{6,5},{7,6},{8,7},{9,8},{10,9},{11,1... | collective-permute-start | bytes 7077896 | tf_op jit(solution)/shard_map/ppermute | solution.py:269
  105.4 62.3 %collective-permute-start.5 = (bf16[384,1536]{1,0:T(8,128)(2,1)}, bf16[384,1536]{1,0:T(8,128)(2,1)}, u32[]{:S(2)}, u32[]{:S(2)}) collective-permute-start(bf16[384,1536]{1,0:T(8,128)(2,1)} %get-tuple-element.50), channel_id=1, source_target_pairs={{0,32},{32,64},{64,96},{1,33},{33,65},{65,97},{2,34},{34,66},{66,9... | collective-permute-start | bytes 3538952 | tf_op jit(solution)/shard_map/ppermute | solution.py:258
  113.6 57.3 %collective-permute-start.6 = (bf16[384,1536]{1,0:T(8,128)(2,1)S(1)}, bf16[384,1536]{1,0:T(8,128)(2,1)}, u32[]{:S(2)}, u32[]{:S(2)}) collective-permute-start(bf16[384,1536]{1,0:T(8,128)(2,1)S(1)} %get-tuple-element.49), channel_id=1, source_target_pairs={{32,0},{64,32},{96,64},{33,1},{65,33},{97,65},{34,2},{66,34},{98,6... | collective-permute-start | bytes 3538952 | tf_op jit(solution)/shard_map/ppermute | solution.py:258
  179.6 93.7 %all-to-all-start.2 = ((bf16[8,5,2,1,32,1536]{5,4,3,2,1,0:T(8,128)(2,1)}), bf16[8,5,2,1,32,1536]{5,4,3,2,1,0:T(8,128)(2,1)}, u32[]{:S(2)}, u32[]{:S(2)}) async-start(bf16[8,5,2,1,32,1536]{5,4,3,2,1,0:T(8,128)(2,1)} %pick_near.1), calls=%async_computation.2 | async-start | bytes 15728640 | tf_op jit(solution)/shard_map/all_to_all | solution.py:275
  184.5 4.7 %copy-start.1 = (bf16[2,1,384,1536]{3,2,1,0:T(8,128)(2,1)S(1)}, bf16[2,1,384,1536]{3,2,1,0:T(8,128)(2,1)}, u32[]{:S(2)}) copy-start(bf16[2,1,384,1536]{3,2,1,0:T(8,128)(2,1)} %param.5) | copy-start | bytes 7077892
  188.6 84.7 %collective-permute-start.7 = (bf16[8,2,2,1,32,1536]{5,4,3,2,1,0:T(8,128)(2,1)}, bf16[8,2,2,1,32,1536]{5,4,3,2,1,0:T(8,128)(2,1)}, u32[]{:S(2)}, u32[]{:S(2)}) collective-permute-start(bf16[8,2,2,1,32,1536]{5,4,3,2,1,0:T(8,128)(2,1)} %slice.95), channel_id=1, source_target_pairs={{0,2},{1,3},{2,0},{3,1},{4,6},{5,7},{6,4},{7,5},{8,10},{9,11},{10,... | collective-permute-start | bytes 9437192 | tf_op jit(solution)/shard_map/ppermute | solution.py:271
  190.8 31.0 %copy-start.6 = (s32[64]{0:T(128)S(1)}, s32[64]{0:T(128)}, u32[]{:S(2)}) copy-start(s32[64]{0:T(128)} %get-tuple-element.62) | copy-start | bytes 772
  214.1 59.3 %collective-permute-start.8 = (bf16[384,1536]{1,0:T(8,128)(2,1)}, bf16[384,1536]{1,0:T(8,128)(2,1)S(1)}, u32[]{:S(2)}, u32[]{:S(2)}) collective-permute-start(bf16[384,1536]{1,0:T(8,128)(2,1)} %get-tuple-element.41), channel_id=1, source_target_pairs={{32,0},{64,32},{96,64},{33,1},{65,33},{97,65},{34,2},{66,34},{98,6... | collective-permute-start | bytes 3538952 | tf_op jit(solution)/shard_map/ppermute | solution.py:291
  216.0 57.3 %collective-permute-start.9 = (bf16[384,1536]{1,0:T(8,128)(2,1)}, bf16[384,1536]{1,0:T(8,128)(2,1)S(1)}, u32[]{:S(2)}, u32[]{:S(2)}) collective-permute-start(bf16[384,1536]{1,0:T(8,128)(2,1)} %get-tuple-element.42), channel_id=1, source_target_pairs={{0,32},{32,64},{64,96},{1,33},{33,65},{65,97},{2,34},{34,66},{66,9... | collective-permute-start | bytes 3538952 | tf_op jit(solution)/shard_map/ppermute | solution.py:292
  222.4 50.2 %collective-permute-start.10 = (f32[384,128]{1,0:T(8,128)}, f32[384,128]{1,0:T(8,128)S(1)}, u32[]{:S(2)}, u32[]{:S(2)}) collective-permute-start(f32[384,128]{1,0:T(8,128)} %get-tuple-element.43), channel_id=1, source_target_pairs={{32,0},{64,32},{96,64},{33,1},{65,33},{97,65},{34,2},{66,34},{98,6... | collective-permute-start | bytes 589832 | tf_op jit(solution)/shard_map/ppermute | solution.py:291
  224.3 49.0 %collective-permute-start.11 = (f32[384,128]{1,0:T(8,128)}, f32[384,128]{1,0:T(8,128)S(1)}, u32[]{:S(2)}, u32[]{:S(2)}) collective-permute-start(f32[384,128]{1,0:T(8,128)} %get-tuple-element.44), channel_id=1, source_target_pairs={{0,32},{32,64},{64,96},{1,33},{33,65},{65,97},{2,34},{34,66},{66,9... | collective-permute-start | bytes 589832 | tf_op jit(solution)/shard_map/ppermute | solution.py:292
  272.6 0.8 copy-start.4
  273.3 0.7 copy-start.5
  273.3 1.1 copy-start.2
  273.3 1.5 copy-start.3

commit v4 on v3

--- a/solution.py
+++ b/solution.py
@@ -27,11 +27,12 @@
     top = functools.reduce(jnp.maximum, [jnp.max(s, axis=1, keepdims=True) for s in scores])
     total = 0.0
     mixed = 0.0
+    shift = top * LOG_SCALE
     for s, v in zip(scores, vals):
-        w = jnp.exp2((s - top) * LOG_SCALE)
+        w = jnp.exp2(s * LOG_SCALE - shift)
         total = total + jnp.sum(w, axis=1, keepdims=True)
         mixed = mixed + dot(w.astype(jnp.bfloat16), v)
-    return mixed / total, top * LOG_SCALE + jnp.log2(total)
+    return mixed / total, shift + jnp.log2(total)
 
 
 def window_kernel(rows_of, place, *refs):
@@ -268,8 +269,8 @@
     k_next, _, _ = lax.optimization_barrier((k, vl, vr))
     kl, kr = lax.ppermute(k_next, "wa", right), lax.ppermute(k_next, "wa", left)
     vl, vr = jnp.where(z == 0, vb, vl), jnp.where(z == DEPTH - 1, vb, vr)
-    far = lax.ppermute(early[:, :2], "wa", across)
-    kl, kr, vl, vr, qu, qd = lax.optimization_barrier((kl, kr, vl, vr, qu, qd))
+    far, kl, kr, vl, vr, qu, qd = lax.optimization_barrier((early[:, :2], kl, kr, vl, vr, qu, qd))
+    far = lax.ppermute(far, "wa", across)
     late = jnp.concatenate([asked_same[:, 0], asked_same[:, 1, 1:], asked_same[:, 2]], axis=1)
     near = pick(late[:, :, None], [kl, vl, kl, vl, k, v, kr, vr, kr, vr], 2, "pick_near")
     near = lax.all_to_all(near, "wa", split_axis=0, concat_axis=0, tiled=True, axis_index_groups=planes)

time: 301 us -> 302 us (level)
  waiting for transfers between devices: 115 us -> 121 us
    ppermute x1, waiting for transfers between devices: 0.01 us -> 49.1 us  [body(): lax.ppermute(v_next, 'wa', spun)]
    ppermute x1, waiting for transfers between devices: 49.2 us -> 2.08 us  [body(): lax.ppermute(v_next, 'wa', spin)]
    ppermute x1, waiting for transfers between devices: 14 us -> 0.01 us  [body(): lax.ppermute(q_next[1], 'ha', down)]
    ppermute x1, waiting for transfers between devices: 3.1 us -> 16.4 us  [body(): lax.ppermute(q_next[0], 'ha', up)]
    ppermute x1, waiting for transfers between devices: 4.13 us -> 8.1 us  [body(): lax.ppermute(edge_level[0], 'ha', up)]
    ppermute x1, starting transfers between devices: 1.92 us -> 5.66 us  [body(): lax.ppermute(q_next[0], 'ha', up)]
    ppermute x1, starting transfers between devices: 8.1 us -> 4.63 us  [body(): lax.ppermute(q_next[1], 'ha', down)]
  transfers between devices with their start and end apart: 15 -> 15, of which waited for: 8 -> 9; matrix products, arithmetic and copies ran while one was open for 8% -> 8% of each run, Pallas kernels for 21% -> 21%
where the time goes in v4:
time: 302 us; the launch traced here: 299 us
  waiting for transfers between devices  121 us (40%)
  Pallas kernels  100 us (33%)
  starting transfers between devices  49.8 us (16%)
  local copies, waits for them, and re-layouts  14.7 us (5%)
  other arithmetic  13.1 us (4%)
    pallas_call x2, Pallas kernels, window(): pl.pallas_call(functools.partial(window_kernel, rows_of), grid_spec=pltpu...  63.5 us
    ppermute x1, waiting for transfers between devices, body(): lax.ppermute(v_next, 'wa', spun)  49.1 us
    ppermute x1, waiting for transfers between devices, body(): vb = lax.ppermute(wrap, 'wa', onto)  27.2 us
    pallas_call x1, Pallas kernels, cubes(): pl.pallas_call(cube_kernel, grid_spec=pltpu.PrefetchScalarGridSpec(num_sc...  21.7 us
    ppermute x1, waiting for transfers between devices, body(): lax.ppermute(q_next[0], 'ha', up)  16.4 us
    pallas_call x2, Pallas kernels, pick(): pl.pallas_call(pick_kernel, grid_spec=pltpu.PrefetchScalarGridSpec(num_sc...  14.7 us
    all_to_all x1, starting transfers between devices, body(): lax.all_to_all(wanted, 'wa', split_axis=0, concat_axis=0, tiled=True)  8.86 us
    ppermute x1, waiting for transfers between devices, body(): lax.ppermute(edge_level[0], 'ha', up)  8.1 us
  transfers between devices with their start and end apart: 15, of which 9 were waited for; matrix products, arithmetic and copies ran while one was open for 8% of the time, Pallas kernels for 21%

profile of v4, /device:TPU:7, one launch (start us, length us, event | category | flops | bytes accessed | tf_op | source)
XLA Modules:
  0.0 299.0 jit_solution(1152583421692814139)
XLA Ops:
  4.2 8.9 %all-to-all-start = ((s32[32,3,2]{1,2,0:T(2,128)}), s32[32,3,2]{1,2,0:T(2,128)S(1)}, u32[]{:S(2)}, u32[]{:S(2)}) async-start(s32[32,3,2]{1,2,0:T(2,128)} %copy.56), calls=%async_computation | async-start | bytes 65536 | tf_op jit(solution)/shard_map/all_to_all | solution.py:257
  13.1 5.6 %all-to-all-done = s32[32,3,2]{1,2,0:T(2,128)S(1)} async-done(((s32[32,3,2]{1,2,0:T(2,128)}), s32[32,3,2]{1,2,0:T(2,128)S(1)}, u32[]{:S(2)}, u32[]{:S(2)}) %all-to-all-start) | async-done | bytes 800 | tf_op jit(solution)/shard_map/all_to_all | solution.py:257
  19.9 6.0 %pick_early.1 = bf16[8,3,2,1,32,1536]{5,4,3,2,1,0:T(8,128)(2,1)} custom-call(s32[8,3,1]{2,1,0:T(4,128)} %copy.58.ids, bf16[24,32,1536]{2,1,0:T(8,128)(2,1)} %bitcast.49, bf16[24,32,1536]{2,1,0:T(8,128)(2,1)} %bitcast.15.refs_1_.refs_3_.refs_5_, bf16[24,32,1536]{2,1,0:T(8,128)(2,1)} %bitcast.50, bf16[24,32,1536]{2,1,0:T(8,128)(2,1)} %bitcast.15.refs_1_.refs_3_.refs_5_, ...), custom_call_target="tpu_custom_call" | custom-call | bytes 9437184 | tf_op jit(solution)/shard_map/pick_early/pallas_call | solution.py:202
  25.8 6.4 %all-to-all-start.1 = ((bf16[8,3,2,1,32,1536]{5,4,3,2,1,0:T(8,128)(2,1)}), bf16[8,3,2,1,32,1536]{5,4,3,2,1,0:T(8,128)(2,1)}, u32[]{:S(2)}, u32[]{:S(2)}) async-start(bf16[8,3,2,1,32,1536]{5,4,3,2,1,0:T(8,128)(2,1)} %pick_early.1), calls=%async_computation.1 | async-start | bytes 9437184 | tf_op jit(solution)/shard_map/all_to_all | solution.py:266
  33.7 49.1 %collective-permute-done.1 = bf16[2,384,1536]{2,1,0:T(8,128)(2,1)} collective-permute-done((bf16[2,384,1536]{2,1,0:T(8,128)(2,1)}, bf16[2,384,1536]{2,1,0:T(8,128)(2,1)}, u32[]{:S(2)}, u32[]{:S(2)}) %collective-permute-start.1) | collective-permute-done | bytes 2359328 | tf_op jit(solution)/shard_map/ppermute | solution.py:260
  84.9 3.3 %broadcast_select_fusion.2 = bf16[2,384,1536]{2,1,0:T(8,128)(2,1)} fusion(bf16[2,384,1536]{2,1,0:T(8,128)(2,1)} %collective-permute-done, bf16[2,384,1536]{2,1,0:T(8,128)(2,1)} %collective-permute-done.1, pred[]{:T(512)S(6)} %eq.96), kind=kLoop, calls=%fused_computation.2 | loop fusion | flops 1179648 | bytes 7077889 | tf_op jit(solution)/shard_map/jit(_where)/select_n | solution.py:267
  88.2 7.7 %all-to-all-done.1.refs_0_.refs_1_ = bf16[8,3,2,1,32,1536]{5,4,3,2,1,0:T(8,128)(2,1)} async-done(((bf16[8,3,2,1,32,1536]{5,4,3,2,1,0:T(8,128)(2,1)}), bf16[8,3,2,1,32,1536]{5,4,3,2,1,0:T(8,128)(2,1)}, u32[]{:S(2)}, u32[]{:S(2)}) %all-to-all-start.1) | async-done | bytes 4718624 | tf_op jit(solution)/shard_map/all_to_all | solution.py:266
  99.9 2.8 slice_bitcast_fusion.2
  102.8 5.7 %collective-permute-start.6 = (bf16[384,1536]{1,0:T(8,128)(2,1)}, bf16[384,1536]{1,0:T(8,128)(2,1)}, u32[]{:S(2)}, u32[]{:S(2)}) collective-permute-start(bf16[384,1536]{1,0:T(8,128)(2,1)} %get-tuple-element.51), channel_id=1, source_target_pairs={{32,0},{64,32},{96,64},{33,1},{65,33},{97,65},{34,2},{66,34},{98,6... | collective-permute-start | bytes 3538952 | tf_op jit(solution)/shard_map/ppermute | solution.py:259
  108.4 4.6 %collective-permute-start.5 = (bf16[384,1536]{1,0:T(8,128)(2,1)S(1)}, bf16[384,1536]{1,0:T(8,128)(2,1)}, u32[]{:S(2)}, u32[]{:S(2)}) collective-permute-start(bf16[384,1536]{1,0:T(8,128)(2,1)S(1)} %get-tuple-element.52), channel_id=1, source_target_pairs={{0,32},{32,64},{64,96},{1,33},{33,65},{65,97},{2,34},{34,66},{66,9... | collective-permute-start | bytes 3538952 | tf_op jit(solution)/shard_map/ppermute | solution.py:259
  116.5 3.9 %slice.93 = bf16[8,2,2,1,32,1536]{5,4,3,2,1,0:T(8,128)(2,1)} slice(bf16[8,3,2,1,32,1536]{5,4,3,2,1,0:T(8,128)(2,1)} %all-to-all-done.1.refs_0_.refs_1_), slice={[0:8], [0:2], [0:2], [0:1], [0:32], [0:1536]} | slice | bytes 6291456 | tf_op jit(solution)/shard_map/slice | solution.py:272
  120.4 27.2 %collective-permute-done.4 = bf16[2,384,1536]{2,1,0:T(8,128)(2,1)} collective-permute-done((bf16[2,384,1536]{2,1,0:T(8,128)(2,1)}, bf16[2,384,1536]{2,1,0:T(8,128)(2,1)}, u32[]{:S(2)}, u32[]{:S(2)}) %collective-permute-start.4) | collective-permute-done | bytes 2359328 | tf_op jit(solution)/shard_map/ppermute | solution.py:268
  147.6 4.9 %broadcast_select_fusion = (bf16[2,384,1536]{2,1,0:T(8,128)(2,1)}, bf16[2,384,1536]{2,1,0:T(8,128)(2,1)}) fusion(bf16[2,384,1536]{2,1,0:T(8,128)(2,1)} %collective-permute-done.4, bf16[2,384,1536]{2,1,0:T(8,128)(2,1)} %collective-permute-done.1, pred[]{:T(512)S(6)} %eq.99, bf16[2,384,1536]{2,1,0:T(8,128)(2,1)} %collective-permute-done, pred[]{:T(512)S(6)} %eq.96), kind=kLoop, calls=%fused_computation | loop fusion | flops 2359296 | bytes 11796482 | tf_op jit(solution)/shard_map/jit(_where)/select_n | solution.py:271
  152.5 16.4 %collective-permute-done.6.refs_1_ = bf16[384,1536]{1,0:T(8,128)(2,1)} collective-permute-done((bf16[384,1536]{1,0:T(8,128)(2,1)}, bf16[384,1536]{1,0:T(8,128)(2,1)}, u32[]{:S(2)}, u32[]{:S(2)}) %collective-permute-start.6) | collective-permute-done | bytes 1179680 | tf_op jit(solution)/shard_map/ppermute | solution.py:259
  168.9 8.7 %pick_near.1 = bf16[8,5,2,1,32,1536]{5,4,3,2,1,0:T(8,128)(2,1)} custom-call(s32[8,5,1]{2,1,0:T(8,128)} %copy.60.ids, bf16[24,32,1536]{2,1,0:T(8,128)(2,1)} %bitcast.23.refs_0_.refs_2_, bf16[24,32,1536]{2,1,0:T(8,128)(2,1)} %bitcast.59, bf16[24,32,1536]{2,1,0:T(8,128)(2,1)} %bitcast.23.refs_0_.refs_2_, bf16[24,32,1536]{2,1,0:T(8,128)(2,1)} %bitcast.60, ...), custom_call_target="tpu_custom_call" | custom-call | bytes 15728640 | tf_op jit(solution)/shard_map/pick_near/pallas_call | solution.py:202
  177.7 5.0 %all-to-all-start.2 = ((bf16[8,5,2,1,32,1536]{5,4,3,2,1,0:T(8,128)(2,1)}), bf16[8,5,2,1,32,1536]{5,4,3,2,1,0:T(8,128)(2,1)}, u32[]{:S(2)}, u32[]{:S(2)}) async-start(bf16[8,5,2,1,32,1536]{5,4,3,2,1,0:T(8,128)(2,1)} %pick_near.1), calls=%async_computation.2 | async-start | bytes 15728640 | tf_op jit(solution)/shard_map/all_to_all | solution.py:276
  184.9 24.3 %window_edge.1 = (bf16[384,1536]{1,0:T(8,128)(2,1)}, bf16[384,1536]{1,0:T(8,128)(2,1)}, f32[384,128]{1,0:T(8,128)}, f32[384,128]{1,0:T(8,128)}) custom-call(s32[2]{0:T(128)} %pad_add_fusion.1.place, bf16[384,1536]{1,0:T(8,128)(2,1)} %collective-permute-done.5.refs_0_, bf16[384,1536]{1,0:T(8,128)(2,1)} %collective-permute-done.6.refs_1_, ...), custom_call_target="tpu_custom_call" | custom-call | flops 5435817984 | bytes 20971520 | tf_op jit(solution)/shard_map/window_edge/pallas_call | solution.py:78
  211.2 5.1 %collective-permute-start.9 = (bf16[384,1536]{1,0:T(8,128)(2,1)}, bf16[384,1536]{1,0:T(8,128)(2,1)S(1)}, u32[]{:S(2)}, u32[]{:S(2)}) collective-permute-start(bf16[384,1536]{1,0:T(8,128)(2,1)} %get-tuple-element.44), channel_id=1, source_target_pairs={{0,32},{32,64},{64,96},{1,33},{33,65},{65,97},{2,34},{34,66},{66,9... | collective-permute-start | bytes 3538952 | tf_op jit(solution)/shard_map/ppermute | solution.py:293
  219.5 5.3 %collective-permute-start.11 = (f32[384,128]{1,0:T(8,128)}, f32[384,128]{1,0:T(8,128)S(1)}, u32[]{:S(2)}, u32[]{:S(2)}) collective-permute-start(f32[384,128]{1,0:T(8,128)} %get-tuple-element.46), channel_id=1, source_target_pairs={{0,32},{32,64},{64,96},{1,33},{33,65},{65,97},{2,34},{34,66},{66,9... | collective-permute-start | bytes 589832 | tf_op jit(solution)/shard_map/ppermute | solution.py:293
  224.8 39.3 %window_own.1 = (f32[384,1536]{1,0:T(8,128)}, f32[384,1536]{1,0:T(8,128)}, f32[384,128]{1,0:T(8,128)}, f32[384,128]{1,0:T(8,128)}) custom-call(s32[2]{0:T(128)} %pad_add_fusion.1.place, bf16[384,1536]{1,0:T(8,128)(2,1)} %get-tuple-element.50.refs_0_, bf16[384,1536]{1,0:T(8,128)(2,1)} %get-tuple-element.49.refs_1_, ...), custom_call_target="tpu_custom_call" | custom-call | flops 10871635968 | bytes 20971520 | tf_op jit(solution)/shard_map/window_own/pallas_call | solution.py:78
  264.1 8.1 %collective-permute-done.10.refs_12_ = f32[384,128]{1,0:T(8,128)S(1)} collective-permute-done((f32[384,128]{1,0:T(8,128)}, f32[384,128]{1,0:T(8,128)S(1)}, u32[]{:S(2)}, u32[]{:S(2)}) %collective-permute-start.10) | collective-permute-done | bytes 196640 | tf_op jit(solution)/shard_map/ppermute | solution.py:292
  272.2 2.4 collective-permute-done.11.refs_13_
  274.6 2.4 all-to-all-done.2
  277.1 21.7 %cubes.1 = bf16[2,384,1536]{2,1,0:T(8,128)(2,1)} custom-call(s32[64]{0:T(128)} %select_reduce_fusion.1.slot_of, s32[2]{0:T(128)} %bitcast.70, s32[2]{0:T(128)} %add_convert_fusion.has, bf16[2,384,1536]{2,1,0:T(8,128)(2,1)} %bitcast.62, bf16[8,3,2,1,32,1536]{5,4,3,2,1,0:T(8,128)(2,1)} %all-to-all-done.1.refs_0_.refs_1_, ...), custom_call_target="tpu_custom_call" | custom-call | flops 4831838208 | bytes 20971520 | tf_op jit(solution)/shard_map/cubes/pallas_call | solution.py:152
  (69 shorter events, 23.7 us)
Async XLA Ops:
  4.2 14.5 %all-to-all-start = ((s32[32,3,2]{1,2,0:T(2,128)}), s32[32,3,2]{1,2,0:T(2,128)S(1)}, u32[]{:S(2)}, u32[]{:S(2)}) async-start(s32[32,3,2]{1,2,0:T(2,128)} %copy.56), calls=%async_computation | async-start | bytes 65536 | tf_op jit(solution)/shard_map/all_to_all | solution.py:257
  25.8 70.0 %all-to-all-start.1 = ((bf16[8,3,2,1,32,1536]{5,4,3,2,1,0:T(8,128)(2,1)}), bf16[8,3,2,1,32,1536]{5,4,3,2,1,0:T(8,128)(2,1)}, u32[]{:S(2)}, u32[]{:S(2)}) async-start(bf16[8,3,2,1,32,1536]{5,4,3,2,1,0:T(8,128)(2,1)} %pick_early.1), calls=%async_computation.1 | async-start | bytes 9437184 | tf_op jit(solution)/shard_map/all_to_all | solution.py:266
  32.2 50.6 %collective-permute-start.1 = (bf16[2,384,1536]{2,1,0:T(8,128)(2,1)}, bf16[2,384,1536]{2,1,0:T(8,128)(2,1)}, u32[]{:S(2)}, u32[]{:S(2)}) collective-permute-start(bf16[2,384,1536]{2,1,0:T(8,128)(2,1)} %bitcast.4.refs_6_), channel_id=1, source_target_pairs={{1,0},{2,1},{3,2},{0,3},{5,4},{6,5},{7,6},{4,7},{9,8},{10,9},{11,1... | collective-permute-start | bytes 7077896 | tf_op jit(solution)/shard_map/ppermute | solution.py:260
  33.2 51.7 %collective-permute-start = (bf16[2,384,1536]{2,1,0:T(8,128)(2,1)}, bf16[2,384,1536]{2,1,0:T(8,128)(2,1)}, u32[]{:S(2)}, u32[]{:S(2)}) collective-permute-start(bf16[2,384,1536]{2,1,0:T(8,128)(2,1)} %bitcast.4.refs_6_), channel_id=1, source_target_pairs={{0,1},{1,2},{2,3},{3,0},{4,5},{5,6},{6,7},{7,4},{8,9},{9,10},{10,1... | collective-permute-start | bytes 7077896 | tf_op jit(solution)/shard_map/ppermute | solution.py:260
  33.7 64.1 %copy-start = (bf16[2,1,384,1536]{3,2,1,0:T(8,128)(2,1)S(1)}, bf16[2,1,384,1536]{3,2,1,0:T(8,128)(2,1)}, u32[]{:S(2)}) copy-start(bf16[2,1,384,1536]{3,2,1,0:T(8,128)(2,1)} %param.6) | copy-start | bytes 7077892
  95.8 51.7 %collective-permute-start.4 = (bf16[2,384,1536]{2,1,0:T(8,128)(2,1)}, bf16[2,384,1536]{2,1,0:T(8,128)(2,1)}, u32[]{:S(2)}, u32[]{:S(2)}) collective-permute-start(bf16[2,384,1536]{2,1,0:T(8,128)(2,1)} %broadcast_select_fusion.2), channel_id=1, source_target_pairs={{0,4},{4,8},{8,12},{12,16},{16,20},{20,24},{24,28},{28,0},{7,3},{1... | collective-permute-start | bytes 7077896 | tf_op jit(solution)/shard_map/ppermute | solution.py:268
  97.8 71.1 %collective-permute-start.3 = (bf16[2,384,1536]{2,1,0:T(8,128)(2,1)S(1)}, bf16[2,384,1536]{2,1,0:T(8,128)(2,1)}, u32[]{:S(2)}, u32[]{:S(2)}) collective-permute-start(bf16[2,384,1536]{2,1,0:T(8,128)(2,1)S(1)} %bitcast.55), channel_id=1, source_target_pairs={{1,0},{2,1},{3,2},{4,3},{5,4},{6,5},{7,6},{8,7},{9,8},{10,9},{11,1... | collective-permute-start | bytes 7077896 | tf_op jit(solution)/shard_map/ppermute | solution.py:270
  98.3 70.6 %collective-permute-start.2 = (bf16[2,384,1536]{2,1,0:T(8,128)(2,1)S(1)}, bf16[2,384,1536]{2,1,0:T(8,128)(2,1)}, u32[]{:S(2)}, u32[]{:S(2)}) collective-permute-start(bf16[2,384,1536]{2,1,0:T(8,128)(2,1)S(1)} %bitcast.56), channel_id=1, source_target_pairs={{0,1},{1,2},{2,3},{3,4},{4,5},{5,6},{6,7},{7,8},{8,9},{9,10},{10,1... | collective-permute-start | bytes 7077896 | tf_op jit(solution)/shard_map/ppermute | solution.py:270
  102.8 66.1 %collective-permute-start.6 = (bf16[384,1536]{1,0:T(8,128)(2,1)}, bf16[384,1536]{1,0:T(8,128)(2,1)}, u32[]{:S(2)}, u32[]{:S(2)}) collective-permute-start(bf16[384,1536]{1,0:T(8,128)(2,1)} %get-tuple-element.51), channel_id=1, source_target_pairs={{32,0},{64,32},{96,64},{33,1},{65,33},{97,65},{34,2},{66,34},{98,6... | collective-permute-start | bytes 3538952 | tf_op jit(solution)/shard_map/ppermute | solution.py:259
  108.4 60.5 %collective-permute-start.5 = (bf16[384,1536]{1,0:T(8,128)(2,1)S(1)}, bf16[384,1536]{1,0:T(8,128)(2,1)}, u32[]{:S(2)}, u32[]{:S(2)}) collective-permute-start(bf16[384,1536]{1,0:T(8,128)(2,1)S(1)} %get-tuple-element.52), channel_id=1, source_target_pairs={{0,32},{32,64},{64,96},{1,33},{33,65},{65,97},{2,34},{34,66},{66,9... | collective-permute-start | bytes 3538952 | tf_op jit(solution)/shard_map/ppermute | solution.py:259
  177.7 5.7 %copy-start.1 = (bf16[2,1,384,1536]{3,2,1,0:T(8,128)(2,1)S(1)}, bf16[2,1,384,1536]{3,2,1,0:T(8,128)(2,1)}, u32[]{:S(2)}) copy-start(bf16[2,1,384,1536]{3,2,1,0:T(8,128)(2,1)} %param.5) | copy-start | bytes 7077892
  177.7 99.4 %all-to-all-start.2 = ((bf16[8,5,2,1,32,1536]{5,4,3,2,1,0:T(8,128)(2,1)}), bf16[8,5,2,1,32,1536]{5,4,3,2,1,0:T(8,128)(2,1)}, u32[]{:S(2)}, u32[]{:S(2)}) async-start(bf16[8,5,2,1,32,1536]{5,4,3,2,1,0:T(8,128)(2,1)} %pick_near.1), calls=%async_computation.2 | async-start | bytes 15728640 | tf_op jit(solution)/shard_map/all_to_all | solution.py:276
  182.7 92.0 %collective-permute-start.7 = (bf16[8,2,2,1,32,1536]{5,4,3,2,1,0:T(8,128)(2,1)}, bf16[8,2,2,1,32,1536]{5,4,3,2,1,0:T(8,128)(2,1)}, u32[]{:S(2)}, u32[]{:S(2)}) collective-permute-start(bf16[8,2,2,1,32,1536]{5,4,3,2,1,0:T(8,128)(2,1)} %slice.93), channel_id=1, source_target_pairs={{0,2},{1,3},{2,0},{3,1},{4,6},{5,7},{6,4},{7,5},{8,10},{9,11},{10,... | collective-permute-start | bytes 9437192 | tf_op jit(solution)/shard_map/ppermute | solution.py:273
  184.9 32.0 %copy-start.6 = (s32[64]{0:T(128)S(1)}, s32[64]{0:T(128)}, u32[]{:S(2)}) copy-start(s32[64]{0:T(128)} %get-tuple-element.64) | copy-start | bytes 772
  209.2 65.4 %collective-permute-start.8 = (bf16[384,1536]{1,0:T(8,128)(2,1)}, bf16[384,1536]{1,0:T(8,128)(2,1)S(1)}, u32[]{:S(2)}, u32[]{:S(2)}) collective-permute-start(bf16[384,1536]{1,0:T(8,128)(2,1)} %get-tuple-element.43), channel_id=1, source_target_pairs={{32,0},{64,32},{96,64},{33,1},{65,33},{97,65},{34,2},{66,34},{98,6... | collective-permute-start | bytes 3538952 | tf_op jit(solution)/shard_map/ppermute | solution.py:292
  211.2 63.5 %collective-permute-start.9 = (bf16[384,1536]{1,0:T(8,128)(2,1)}, bf16[384,1536]{1,0:T(8,128)(2,1)S(1)}, u32[]{:S(2)}, u32[]{:S(2)}) collective-permute-start(bf16[384,1536]{1,0:T(8,128)(2,1)} %get-tuple-element.44), channel_id=1, source_target_pairs={{0,32},{32,64},{64,96},{1,33},{33,65},{65,97},{2,34},{34,66},{66,9... | collective-permute-start | bytes 3538952 | tf_op jit(solution)/shard_map/ppermute | solution.py:293
  217.6 54.6 %collective-permute-start.10 = (f32[384,128]{1,0:T(8,128)}, f32[384,128]{1,0:T(8,128)S(1)}, u32[]{:S(2)}, u32[]{:S(2)}) collective-permute-start(f32[384,128]{1,0:T(8,128)} %get-tuple-element.45), channel_id=1, source_target_pairs={{32,0},{64,32},{96,64},{33,1},{65,33},{97,65},{34,2},{66,34},{98,6... | collective-permute-start | bytes 589832 | tf_op jit(solution)/shard_map/ppermute | solution.py:292
  219.5 55.1 %collective-permute-start.11 = (f32[384,128]{1,0:T(8,128)}, f32[384,128]{1,0:T(8,128)S(1)}, u32[]{:S(2)}, u32[]{:S(2)}) collective-permute-start(f32[384,128]{1,0:T(8,128)} %get-tuple-element.46), channel_id=1, source_target_pairs={{0,32},{32,64},{64,96},{1,33},{33,65},{65,97},{2,34},{34,66},{66,9... | collective-permute-start | bytes 589832 | tf_op jit(solution)/shard_map/ppermute | solution.py:293
  272.2 4.9 %copy-start.4 = (f32[384,128]{1,0:T(8,128)}, f32[384,128]{1,0:T(8,128)S(1)}, u32[]{:S(2)}) copy-start(f32[384,128]{1,0:T(8,128)S(1)} %collective-permute-done.10.refs_12_) | copy-start | bytes 589828
  274.6 2.5 copy-start.5
  274.6 2.5 copy-start.2
  274.6 2.5 copy-start.3
